TPU v7x, 512 devices: a whole 4x4x16 slice. The times are simulated.
512 devices in a mesh: tm: 16 (over z_lo, x), ctx: 32 (over y, z_hi, core).
Axes of the slice: x: 4, y: 4, z: 16 (z_hi: 4, z_lo: 4; z = z_hi * 4 + z_lo), core: 2. Of those that a mesh axis runs over, the one named last changes fastest.
Arguments:
- states: float32 [16, 3072, 64], P('tm', 'ctx'), may hold values from -6 to 6
- noise_draws: float32 [16, 3072, 64], P('tm', 'ctx'), may hold values from -6 to 6
- plan: int32 [17], replicated, may hold values from 0 to 1000, as said below
- w_embed: bfloat16 [64, 3072], replicated, may hold values from -0.75 to 0.75
- w_time: bfloat16 [128, 3072], replicated, may hold values from -0.5 to 0.5
- w_query: bfloat16 [16, 3072, 128], P('tm'), may hold values from -0.109375 to 0.109375
- w_key: bfloat16 [16, 3072, 128], P('tm'), may hold values from -0.109375 to 0.109375
- w_value: bfloat16 [16, 3072, 128], P('tm'), may hold values from -0.109375 to 0.109375
- gain_query: float32 [16, 128], P('tm'), may hold values from 0.5 to 16, as said below
- gain_key: float32 [16, 128], P('tm'), may hold values from 0.5 to 16, as said below
- w_out: bfloat16 [16, 128, 3072], P('tm'), may hold values from -0.5 to 0.5
- w_final: bfloat16 [3072, 64], replicated, may hold values from -0.109375 to 0.109375
Outputs:
- new_states: float32 [16, 3072, 64], P('tm', 'ctx')
Inputs may be any that keep to these rules, and one draw needn't show every extreme that they name: plan[0] is 1000 and each later entry is smaller than the one before by 31 to 61. `gain_query`: positive gains. `gain_key`: positive gains.
All inputs are finite; a program needn't handle non-finite values.
Results may differ from a plain program's by a relative error of at most 0.014.
The roundings to bfloat16 on the way count: a program that leaves them out, or rounds other values in their place, can miss the bound.
Values may be sent and summed in bfloat16 or wider, within the bound.
No kernel may reach another device: no remote copies, remote signals or barrier semaphores. Data moves between devices by JAX's collectives and lax.ppermute only.
A program may use at most 64 MiB of HBM per device.

v0:
```python
import math

import jax
import jax.numpy as jnp
from jax import lax
from jax.sharding import PartitionSpec as P


def with_halo(array, sides, width):
    for axis, dim in sides:
        size, length = (lax.axis_size(axis), array.shape[dim])
        up = [(i, (i + 1) % size) for i in range(size - 1)]
        down = [(j, i) for i, j in up]
        last = lax.slice_in_dim(array, length - width, length, axis=dim)
        first = lax.slice_in_dim(array, 0, width, axis=dim)
        before = lax.ppermute(last, axis, up)
        after = lax.ppermute(first, axis, down)
        array = jnp.concatenate([before, array, after], axis=dim)
    return array


def entering(value, axis, join, neutral):
    count, mine = (lax.axis_size(axis), lax.axis_index(axis))
    pieces = lax.all_gather(value, axis)
    total = jnp.full_like(value, 0) + jnp.asarray(neutral, value.dtype)

    def hop(position, total):
        longer = join(total, pieces[position])
        return jnp.where(position < mine, longer, total)

    return lax.fori_loop(0, count - 1, hop, total)


def fourier_rows(plan, freq_count, step_count):
    half_freq = freq_count // 2
    frequency = jnp.exp(-math.log(10000.0) * jnp.arange(half_freq, dtype=jnp.float32) / half_freq)
    phase_arg = plan[:step_count].astype(jnp.float32)[:, None] * frequency[None, :]
    return jnp.concatenate([jnp.cos(phase_arg), jnp.sin(phase_arg)], axis=1).astype(jnp.bfloat16)


def rms_gain(values_in, gain_row):
    scale = lax.rsqrt(jnp.mean(values_in * values_in, axis=-1, keepdims=True) + 1e-06)
    return values_in * scale * gain_row


def per_device(
    states,
    noise_draws,
    plan,
    w_embed,
    w_time,
    w_query,
    w_key,
    w_value,
    gain_query,
    gain_key,
    w_out,
    w_final,
):
    every = lax.all_gather(states, "tm", axis=0, tiled=True)
    nsteps, tok_rows, channels = every.shape
    own_steps = states.shape[0]
    model_width = w_embed.shape[1]
    head_dim = w_query.shape[2]
    ctx_count = lax.axis_size("ctx")
    ctx_index = lax.axis_index("ctx")
    tm_index = lax.axis_index("tm")
    features = fourier_rows(plan, w_time.shape[0], nsteps)
    time_shift = jnp.dot(features, w_time, preferred_element_type=jnp.float32)
    latents = every.astype(jnp.bfloat16)
    count = latents.shape[1]
    embedded = jnp.dot(
        latents.reshape(nsteps * count, channels), w_embed, preferred_element_type=jnp.float32
    )
    hidden = (embedded.reshape(nsteps, count, model_width) + time_shift[:, None, :]).astype(
        jnp.bfloat16
    )
    count = hidden.shape[1]
    flat_rows = hidden.reshape(nsteps * count, model_width)
    key_rows = rms_gain(
        jnp.dot(flat_rows, w_key[0], preferred_element_type=jnp.float32), gain_key[0]
    ).astype(jnp.bfloat16)
    value_rows = jnp.dot(flat_rows, w_value[0], preferred_element_type=jnp.float32).astype(
        jnp.bfloat16
    )
    key_value = with_halo(
        jnp.concatenate([key_rows, value_rows], axis=1).reshape(nsteps, count, 2 * head_dim),
        (("ctx", 1),),
        tok_rows,
    )
    flat_hidden = hidden.reshape(nsteps * tok_rows, model_width)
    queries = rms_gain(
        jnp.dot(flat_hidden, w_query[0], preferred_element_type=jnp.float32), gain_query[0]
    ).astype(jnp.bfloat16)
    queries = queries.reshape(nsteps, tok_rows, head_dim)
    key_part = key_value[..., :head_dim]
    value_part = key_value[..., head_dim:]
    block_of = jnp.arange(3 * tok_rows, dtype=jnp.int32) // tok_rows
    valid = (
        (block_of == 1)
        | (block_of == 0) & (ctx_index > 0)
        | (block_of == 2) & (ctx_index < ctx_count - 1)
    )
    valid = valid[None, None, :]
    scores = jnp.einsum(
        "sqe,ske->sqk", queries, key_part, preferred_element_type=jnp.float32
    ) / math.sqrt(head_dim)
    top_score = jnp.max(jnp.where(valid, scores, -1e30), axis=-1, keepdims=True)
    expo = jnp.where(valid, jnp.exp(scores - top_score), 0.0)
    attn_probs = (expo / jnp.sum(expo, axis=-1, keepdims=True)).astype(jnp.bfloat16)
    attended = jnp.einsum(
        "sqk,ske->sqe", attn_probs, value_part, preferred_element_type=jnp.float32
    ).astype(jnp.bfloat16)
    projected = jnp.dot(
        attended.reshape(nsteps * tok_rows, head_dim), w_out[0], preferred_element_type=jnp.float32
    ).astype(jnp.bfloat16)
    head_terms = jnp.dot(projected, w_final, preferred_element_type=jnp.float32).reshape(
        nsteps, tok_rows, channels
    )
    own_hidden = lax.dynamic_slice_in_dim(hidden, tm_index * own_steps, own_steps, 0)
    residual = jnp.dot(
        own_hidden.reshape(own_steps * tok_rows, model_width),
        w_final,
        preferred_element_type=jnp.float32,
    )
    residual = residual.reshape(own_steps, tok_rows, channels)
    step_sizes = (plan[:-1] - plan[1:]).astype(jnp.float32) / 1000.0
    own_sizes = lax.dynamic_slice_in_dim(step_sizes, tm_index * own_steps, own_steps, 0)
    start_state = every[0][None, :, :]
    drift_rows = lax.psum_scatter(head_terms, "tm", scatter_dimension=0, tiled=True) + residual
    increment = (
        own_sizes[:, None, None] * drift_rows + jnp.sqrt(own_sizes)[:, None, None] * noise_draws
    )
    running = jnp.cumsum(increment, axis=0)
    earlier = entering(running[-1], "tm", jnp.add, jnp.zeros_like(running[-1]))
    return start_state + earlier[None, :, :] + running


def solution(mesh):
    return jax.shard_map(
        per_device,
        mesh=mesh,
        in_specs=(
            P("tm", "ctx", None),
            P("tm", "ctx", None),
            P(),
            P(),
            P(),
            P("tm", None, None),
            P("tm", None, None),
            P("tm", None, None),
            P("tm", None),
            P("tm", None),
            P("tm", None, None),
            P(),
        ),
        out_specs=P("tm", "ctx", None),
        check_vma=False,
    )
```

profile of v0, /device:TPU:8, one launch (start us, length us, event | category | flops | bytes accessed | tf_op | source)
XLA Modules:
  0.0 257.8 jit_solution(12405270481454556288)
XLA Ops:
  6.5 0.0 copy-start
  6.5 0.0 reduce-scatter.2.cloned.1.call-start
  6.5 0.7 slice_convert_fusion
  7.3 46.7 %all_gather.6 = f32[16,96,64]{1,2,0:T(8,128)S(1)} all-gather(f32[1,96,64]{1,2,0:T(8,128)} %param.14), channel_id=1, replica_groups=mesh['tm'=16,'ctx'=32] {'tm'}, dimensions={0}, use_global_device_ids=true | all-gather | bytes 417792 | tf_op jit(solution)/shard_map/all_gather | solution.py:60
  54.0 0.1 fusion.27
  54.1 1.4 fusion.29
  55.5 3.9 %add_convert_fusion = bf16[16,96,3072]{2,1,0:T(8,128)(2,1)S(1)} fusion(f32[16,3072]{1,0:T(8,128)S(1)} %fusion.29, bf16[64,3072]{1,0:T(8,128)(2,1)} %param.17, f32[16,96,64]{1,2,0:T(8,128)S(1)} %all_gather.6), kind=kOutput, calls=%fused_computation.3 | convolution fusion | flops 613515264 | bytes 10420224 | tf_op jit(solution)/shard_map/dot_general | solution.py:72
  59.4 0.0 copy-start.1
  59.4 0.0 copy-done
  59.4 0.0 copy-start.2
  59.4 3.3 %multiply_reduce_fusion = (f32[1536]{0:T(1024)S(1)}, f32[1536,128]{0,1:T(8,128)S(1)}) fusion(bf16[1536,3072]{1,0:T(8,128)(2,1)S(1)} %bitcast.55, bf16[1,3072,128]{2,1,0:T(8,128)(2,1)S(1)} %copy-done), kind=kOutput, calls=%fused_computation.32 | convolution fusion | flops 1208351232 | bytes 11016192 | tf_op jit(solution)/shard_map/dot_general | solution.py:81
  62.7 0.3 copy-done.1
  63.0 0.0 copy-done.2
  63.0 3.3 %convolution_convert_fusion.1 = bf16[1536,128]{0,1:T(8,128)(2,1)S(1)} fusion(bf16[1536,3072]{1,0:T(8,128)(2,1)S(1)} %bitcast.56, bf16[1,3072,128]{2,1,0:T(8,128)(2,1)S(1)} %copy-done.2), kind=kOutput, calls=%fused_computation.6 | convolution fusion | flops 1208156160 | bytes 10616832 | tf_op jit(solution)/shard_map/dot_general | solution.py:83
  66.3 0.0 copy-done.5
  66.3 0.1 multiply_convert_fusion
  66.4 0.1 pad_maximum_fusion.1
  66.5 0.3 copy.22
  66.7 1.9 collective-permute-start
  68.7 8.6 %collective-permute-start.1 = (bf16[16,96,256]{2,1,0:T(8,128)(2,1)S(1)}, bf16[16,96,256]{2,1,0:T(8,128)(2,1)}, u32[]{:S(2)}, u32[]{:S(2)}) collective-permute-start(bf16[16,96,256]{2,1,0:T(8,128)(2,1)S(1)} %bitcast.59), channel_id=1, source_target_pairs={{1,0},{2,1},{3,2},{4,3},{5,4},{6,5},{7,6},{8,7},{9,8},{10,9},{11,1... | collective-permute-start | bytes 2359304 | tf_op jit(solution)/shard_map/ppermute | solution.py:17
  77.3 0.0 copy-start.6
  77.3 5.5 %multiply_reduce_fusion.1 = (f32[1536]{0:T(1024)S(1)}, f32[1536,128]{1,0:T(8,128)S(1)}) fusion(bf16[1536,3072]{1,0:T(8,128)(2,1)} %bitcast.57, bf16[1,3072,128]{2,1,0:T(8,128)(2,1)} %param.19), kind=kOutput, calls=%fused_computation.34 | convolution fusion | flops 1208351232 | bytes 11016192 | tf_op jit(solution)/shard_map/dot_general | solution.py:93
  82.9 0.0 copy-done.6
  82.9 0.3 multiply_convert_fusion.1
  83.2 24.8 %collective-permute-done = bf16[16,96,256]{2,1,0:T(8,128)(2,1)} collective-permute-done((bf16[16,96,256]{2,1,0:T(8,128)(2,1)S(1)}, bf16[16,96,256]{2,1,0:T(8,128)(2,1)}, u32[]{:S(2)}, u32[]{:S(2)}) %collective-permute-start) | collective-permute-done | bytes 786464 | tf_op jit(solution)/shard_map/ppermute | solution.py:16
  107.9 0.0 collective-permute-done.1
  107.9 1.5 pad_maximum_fusion
  109.5 0.7 fusion.7
  110.2 1.0 fusion.40
  111.1 0.0 copy-start.3
  111.2 0.0 copy-start.7
  111.2 0.6 convolution_convert_fusion.2
  111.8 0.3 copy-done.3
  112.1 0.3 copy-done.7
  112.4 5.4 %fusion.1 = f32[1536,64]{0,1:T(8,128)S(1)} fusion(bf16[3072,64]{0,1:T(8,128)(2,1)S(1)} %copy-done.3, bf16[1536,128]{1,0:T(8,128)(2,1)S(1)} %bitcast.64, bf16[1,128,3072]{2,1,0:T(8,128)(2,1)S(1)} %copy-done.7), kind=kOutput, calls=%fused_computation.5 | convolution fusion | flops 1816657920 | bytes 1966080 | tf_op jit(solution)/shard_map/dot_general | solution.py:117
  117.8 0.0 copy-start.8
  117.8 0.0 copy-start.4
  117.8 0.2 reshape.81
  118.0 0.9 copy.23
  118.9 0.0 reduce-scatter.2.cloned.1.call-update
  118.9 0.0 copy-done.8
  119.0 0.1 convert_multiply_fusion
  119.0 0.6 dynamic_slice.13
  120.2 85.3 %reduce-scatter.2.cloned.1.call-done = f32[1,96,64]{1,2,0:T(8,128)} async-done(((f32[16,96,64]{1,2,0:T(8,128)}), f32[1,96,64]{1,2,0:T(8,128)}) %reduce-scatter.2.cloned.1.call-update) | async-done | bytes 24592 | tf_op jit(solution)/shard_map/reduce_scatter | solution.py:130
  205.5 1.9 fusion.14
  207.5 40.5 %all_gather.7 = f32[16,96,64]{1,2,0:T(8,128)S(1)} all-gather(f32[1,96,64]{1,2,0:T(8,128)S(1)} %fusion.14), channel_id=1, replica_groups=mesh['tm'=16,'ctx'=32] {'tm'}, dimensions={0}, use_global_device_ids=true | all-gather | bytes 417792 | tf_op jit(solution)/shard_map/all_gather | solution.py:24
  248.0 2.2 while.14
  248.0 0.1 copy.28
  248.2 0.1 copy.28
  248.3 0.1 copy.28
  248.5 0.1 copy.28
  248.6 0.1 copy.28
  248.8 0.1 copy.28
  248.9 0.1 copy.28
  249.1 0.1 copy.28
  249.2 0.1 copy.28
  249.4 0.1 copy.28
  249.5 0.1 copy.28
  249.7 0.1 copy.28
  249.8 0.1 copy.28
  250.0 0.1 copy.28
  250.1 0.1 copy.28
  250.2 0.1 copy.25
  250.3 0.6 fusion.26
  (37 shorter events, 0.4 us)
Async XLA Ops:
  6.5 52.9 %copy-start = (bf16[1,3072,128]{2,1,0:T(8,128)(2,1)S(1)}, bf16[1,3072,128]{2,1,0:T(8,128)(2,1)}, u32[]{:S(2)}) copy-start(bf16[1,3072,128]{2,1,0:T(8,128)(2,1)} %param.20) | copy-start | bytes 2359300
  6.5 199.0 %reduce-scatter.2.cloned.1.call-start = ((), (), s32[]{:S(2)}) async-start(), calls=%async_computation.1 | async-start | bytes 557056 | tf_op jit(solution)/shard_map/reduce_scatter | solution.py:130
  59.4 3.6 %copy-start.1 = (bf16[16,96,3072]{2,1,0:T(8,128)(2,1)}, bf16[16,96,3072]{2,1,0:T(8,128)(2,1)S(1)}, u32[]{:S(2)}) copy-start(bf16[16,96,3072]{2,1,0:T(8,128)(2,1)S(1)} %add_convert_fusion) | copy-start | bytes 28311556
  59.4 3.6 %copy-start.2 = (bf16[1,3072,128]{2,1,0:T(8,128)(2,1)S(1)}, bf16[1,3072,128]{2,1,0:T(8,128)(2,1)}, u32[]{:S(2)}) copy-start(bf16[1,3072,128]{2,1,0:T(8,128)(2,1)} %param.21) | copy-start | bytes 2359300
  63.0 3.3 %copy-start.5 = (f32[1,128]{1,0:T(1,128)S(1)}, f32[1,128]{1,0:T(1,128)}, u32[]{:S(2)}) copy-start(f32[1,128]{1,0:T(1,128)} %param.23) | copy-start | bytes 1540
  66.7 41.2 %collective-permute-start = (bf16[16,96,256]{2,1,0:T(8,128)(2,1)S(1)}, bf16[16,96,256]{2,1,0:T(8,128)(2,1)}, u32[]{:S(2)}, u32[]{:S(2)}) collective-permute-start(bf16[16,96,256]{2,1,0:T(8,128)(2,1)S(1)} %bitcast.58), channel_id=1, source_target_pairs={{0,1},{1,2},{2,3},{3,4},{4,5},{5,6},{6,7},{7,8},{8,9},{9,10},{10,1... | collective-permute-start | bytes 2359304 | tf_op jit(solution)/shard_map/ppermute | solution.py:16
  68.7 39.3 %collective-permute-start.1 = (bf16[16,96,256]{2,1,0:T(8,128)(2,1)S(1)}, bf16[16,96,256]{2,1,0:T(8,128)(2,1)}, u32[]{:S(2)}, u32[]{:S(2)}) collective-permute-start(bf16[16,96,256]{2,1,0:T(8,128)(2,1)S(1)} %bitcast.59), channel_id=1, source_target_pairs={{1,0},{2,1},{3,2},{4,3},{5,4},{6,5},{7,6},{8,7},{9,8},{10,9},{11,1... | collective-permute-start | bytes 2359304 | tf_op jit(solution)/shard_map/ppermute | solution.py:17
  77.3 5.5 %copy-start.6 = (f32[1,128]{1,0:T(1,128)S(1)}, f32[1,128]{1,0:T(1,128)}, u32[]{:S(2)}) copy-start(f32[1,128]{1,0:T(1,128)} %param.22) | copy-start | bytes 1540
  111.1 1.0 copy-start.3
  111.2 1.2 copy-start.7
  117.8 1.2 copy-start.8
  117.8 87.8 %copy-start.4 = (f32[1,96,64]{1,2,0:T(8,128)S(1)}, f32[1,96,64]{1,2,0:T(8,128)}, u32[]{:S(2)}) copy-start(f32[1,96,64]{1,2,0:T(8,128)} %param.15) | copy-start | bytes 73732
Sparse Core Ops, SparseCore 0:
  119.1 86.4 reduce-scatter.1
where the time goes:
time: 258 us
  waiting for transfers between devices  110 us (43%)
  blocking collectives  87.3 us (34%)
  matrix products  25.9 us (10%)
  between operations  14.2 us (6%)
  starting transfers between devices  10.6 us (4%)
  other arithmetic  4.76 us (2%)
  local copies, waits for them, and re-layouts  4.32 us (2%)
    reduce_scatter x1, waiting for transfers between devices, per_device(): lax.psum_scatter(head_terms, 'tm', scatter_dimension=0, tiled=True)  85.3 us
    all_gather x1, blocking collectives, per_device(): every = lax.all_gather(states, 'tm', axis=0, tiled=True)  46.7 us
    all_gather x1, blocking collectives, entering(): pieces = lax.all_gather(value, axis)  40.5 us
    ppermute x1, waiting for transfers between devices, with_halo(): before = lax.ppermute(last, axis, up)  24.8 us
    ppermute x1, starting transfers between devices, with_halo(): after = lax.ppermute(first, axis, down)  8.63 us
    dot_general x1, matrix products, per_device(): jnp.dot(flat_hidden, w_query[0], preferred_element_type=jnp.float32)  5.49 us
    dot_general x1, matrix products, per_device(): jnp.dot(projected, w_final, preferred_element_type=jnp.float32)  5.35 us
  transfers between devices with their start and end apart: 3, of which 2 were waited for; matrix products, arithmetic and copies ran while one was open for 2% of the time, Pallas kernels for 0%

commit v1 on v0

v1 whole, which is shorter than its diff:
```python
import functools
import math

import jax
import jax.numpy as jnp
from jax import lax
from jax.experimental import pallas as pl
from jax.experimental.pallas import tpu as pltpu
from jax.sharding import PartitionSpec as P

F32, BF16 = jnp.float32, jnp.bfloat16
MIB = 1 << 20
VMEM = pl.BlockSpec(memory_space=pltpu.VMEM)
ANY = pl.BlockSpec(memory_space=pl.ANY)
SMEM = pl.BlockSpec(memory_space=pltpu.SMEM)
NT = (((1,), (1,)), ((), ()))


def fourier_rows(plan, freq_count, step_count):
    half_freq = freq_count // 2
    frequency = jnp.exp(-math.log(10000.0) * jnp.arange(half_freq, dtype=F32) / half_freq)
    phase_arg = plan[:step_count].astype(F32)[:, None] * frequency[None, :]
    return jnp.concatenate([jnp.cos(phase_arg), jnp.sin(phase_arg)], axis=1).astype(BF16)


def dot(a, b):
    return jnp.dot(a, b, preferred_element_type=F32)


def split(value):
    high = value.astype(BF16)
    return high, (value - high.astype(F32)).astype(BF16)


def pack_kernel(state_ref, copies_ref):
    rows = state_ref[...].T.astype(BF16)
    half = rows.shape[0] // 2
    packed = jnp.concatenate([rows[:half], rows[half:]], axis=1)
    copies_ref[...] = jnp.broadcast_to(packed[None], copies_ref.shape)


def fold_kernel(embed_ref, time_ref, value_ref, out_ref, final_ref, into_value, into_final, tail):
    freq, width = time_ref.shape[0], value_ref.shape[1]
    channels = final_ref.shape[0]
    final = final_ref[...]
    for rows, ref in (((0, freq), time_ref), ((freq, freq + embed_ref.shape[0]), embed_ref)):
        left = ref[...]
        high, low = split(dot(left, value_ref[...]))
        into_value[rows[0] : rows[1], :width] = high
        into_value[rows[0] : rows[1], width:] = low
        product = lax.dot_general(left, final, NT, preferred_element_type=F32)
        into_final[rows[0] : rows[1], :] = jnp.concatenate(split(product), axis=1)
    product = lax.dot_general(out_ref[...], final, NT, preferred_element_type=F32)
    tail[...] = jnp.concatenate(split(product), axis=1)


def rms_gain(values, gain):
    scale = lax.rsqrt(jnp.mean(values * values, axis=-1, keepdims=True) + 1e-06)
    return values * scale * gain


def fill_inputs(latent_ref, feature_ref, inputs):
    steps, half, both = latent_ref.shape
    channels, freq = both // 2, feature_ref.shape[1]
    for s in range(steps):
        row = s * 2 * half
        packed = latent_ref[s]
        inputs[row : row + half, freq:] = packed[:, :channels]
        inputs[row + half : row + 2 * half, freq:] = packed[:, channels:]
        inputs[row : row + 2 * half, :freq] = jnp.broadcast_to(
            feature_ref[s : s + 1, :], (2 * half, freq)
        )


def project_kernel(
    own,
    block,
    chunk,
    latent_ref,
    feature_ref,
    embed_ref,
    time_ref,
    left_ref,
    right_ref,
    *rest,
):
    if own:
        into_value, gain_query, gain_key, query_out, pair_out = rest[:5]
    else:
        gain_key, pair_out = rest[:2]
    inputs, first, second, sems = rest[-4:]
    freq, width = time_ref.shape[0], left_ref.shape[1]
    copies = [
        pltpu.make_async_copy(time_ref, first.at[:freq], sems.at[0]),
        pltpu.make_async_copy(embed_ref, first.at[freq:], sems.at[1]),
        pltpu.make_async_copy(left_ref, second.at[:, :width], sems.at[2]),
        pltpu.make_async_copy(right_ref, second.at[:, width:], sems.at[3]),
    ]
    for copy in copies:
        copy.start()
    fill_inputs(latent_ref, feature_ref, inputs)
    for copy in copies:
        copy.wait()
    rows, depth = inputs.shape[0], first.shape[1]

    def step(i, carry):
        here = pl.ds(pl.multiple_of(i * block, block), block)
        taken = inputs[here, :]
        total = None
        for n in range(0, depth, chunk):
            hidden = dot(taken, first[:, n : n + chunk]).astype(BF16)
            part = dot(hidden, second[n : n + chunk, :])
            total = part if total is None else total + part
        if own:
            query_out[here, :] = rms_gain(total[:, :width], gain_query[...]).astype(BF16)
            pair_out[here, :width] = rms_gain(total[:, width:], gain_key[...]).astype(BF16)
            values = dot(taken, into_value[...])
            pair_out[here, width:] = (values[:, :width] + values[:, width:]).astype(BF16)
        else:
            pair_out[here, :width] = rms_gain(total[:, :width], gain_key[...]).astype(BF16)
            pair_out[here, width:] = total[:, width:].astype(BF16)
        return carry

    lax.fori_loop(0, rows // block, step, 0)


def attend_kernel(
    plan_ref,
    query_ref,
    own_ref,
    inner_ref,
    outer_ref,
    tail_ref,
    latent_ref,
    feature_ref,
    into_final,
    state_ref,
    noise_ref,
    sent_ref,
):
    steps, half, both = sent_ref.shape
    channels, tile = both // 2, 2 * half
    width = query_ref.shape[1]
    mine, place = lax.axis_index("tm"), lax.axis_index("ctx")
    alone = (place == 0) | (place == lax.axis_size("ctx") - 1)
    scale = 1.0 / math.sqrt(width)

    def size_of(s):
        return (plan_ref[s] - plan_ref[s + 1]).astype(F32) / 1000.0

    own_size = jnp.full((tile, channels), size_of(mine), F32)
    packed = latent_ref[mine]
    rows = jnp.concatenate([packed[:, :channels], packed[:, channels:]], axis=0)
    features = feature_ref[...].astype(F32)
    chosen = lax.broadcasted_iota(jnp.int32, features.shape, 0) == mine
    features = jnp.sum(jnp.where(chosen, features, 0.0), axis=0, keepdims=True).astype(BF16)
    features = jnp.broadcast_to(features, (tile, features.shape[1]))
    taken = jnp.concatenate([features, rows], axis=1)
    residual = dot(taken, into_final[...])
    extra = own_size * (residual[:, :channels] + residual[:, channels:])
    extra = extra + jnp.sqrt(own_size) * noise_ref[...].T
    extra = extra + jnp.where(mine == 0, state_ref[...].T, 0.0)
    column = lax.broadcasted_iota(jnp.int32, (tile, 3 * tile), 1)
    hidden_key = (column >= 2 * tile) & alone

    running = jnp.zeros((tile, channels), F32)
    for s in range(steps):
        here = slice(s * tile, (s + 1) * tile)
        keys = jnp.concatenate([r[here, :width] for r in (own_ref, inner_ref, outer_ref)], axis=0)
        values = jnp.concatenate([r[here, width:] for r in (own_ref, inner_ref, outer_ref)], axis=0)
        scores = lax.dot_general(query_ref[here, :], keys, NT, preferred_element_type=F32) * scale
        scores = jnp.where(hidden_key, -1e30, scores)
        expo = jnp.exp(scores - jnp.max(scores, axis=-1, keepdims=True))
        probs = (expo * (1.0 / jnp.sum(expo, axis=-1, keepdims=True))).astype(BF16)
        attended = dot(probs, values).astype(BF16)
        terms = dot(attended, tail_ref[...])
        running = running + size_of(s) * (terms[:, :channels] + terms[:, channels:])
        total = running + jnp.where(s >= mine, extra, 0.0)
        sent_ref[s] = jnp.concatenate([total[:half], total[half:]], axis=1).astype(BF16)


def sum_kernel(taken_ref, out_ref):
    total = jnp.sum(taken_ref[...].astype(F32), axis=0)
    channels = total.shape[1] // 2
    out_ref[...] = jnp.concatenate([total[:, :channels], total[:, channels:]], axis=0).T


def call(kernel, shapes, specs, scratch=(), limit=24, flops=0, moved=0):
    many = isinstance(shapes, (list, tuple))
    return pl.pallas_call(
        kernel,
        out_shape=shapes,
        in_specs=specs,
        out_specs=[VMEM] * len(shapes) if many else VMEM,
        scratch_shapes=list(scratch),
        compiler_params=pltpu.CompilerParams(vmem_limit_bytes=limit * MIB),
        cost_estimate=pl.CostEstimate(flops=flops, bytes_accessed=moved, transcendentals=0),
    )


def struct(shape, dtype):
    return jax.ShapeDtypeStruct(shape, dtype)


def per_device(
    states,
    noise_draws,
    plan,
    w_embed,
    w_time,
    w_query,
    w_key,
    w_value,
    gain_query,
    gain_key,
    w_out,
    w_final,
):
    steps = lax.axis_size("tm")
    tile, channels = states.shape[1:]
    freq, depth = w_time.shape
    width = w_query.shape[2]
    count = lax.axis_size("ctx")
    rows = steps * tile
    state, noise = states[0].T, noise_draws[0].T
    final = w_final.T
    packed = (steps, tile // 2, 2 * channels)
    features = fourier_rows(plan, freq, steps)

    copies = call(pack_kernel, struct(packed, BF16), [VMEM], limit=8)(state)
    latents = lax.all_to_all(copies, "tm", 0, 0, tiled=True)
    outward = [(i, i + 1 if i % 2 else i - 1) for i in range(1, count - 1)]
    outer_latents = lax.ppermute(latents, "ctx", outward)
    into_value, into_final, tail = call(
        fold_kernel,
        [
            struct((freq + channels, 2 * width), BF16),
            struct((freq + channels, 2 * channels), BF16),
            struct((width, 2 * channels), BF16),
        ],
        [VMEM] * 5,
    )(w_embed, w_time, w_value[0], w_out[0], final)
    scratch = [
        pltpu.VMEM((rows, freq + channels), BF16),
        pltpu.VMEM((freq + channels, depth), BF16),
        pltpu.VMEM((depth, 2 * width), BF16),
        pltpu.SemaphoreType.DMA((4,)),
    ]
    block, chunk = 4 * tile, 512
    flops = 4 * rows * depth * 256
    query, own_pair = call(
        functools.partial(project_kernel, True, block, chunk),
        [struct((rows, width), BF16), struct((rows, 2 * width), BF16)],
        [VMEM, VMEM] + [ANY] * 4 + [VMEM] * 3,
        scratch,
        flops=flops,
        moved=4 * MIB,
    )(latents, features, w_embed, w_time, w_query[0], w_key[0], into_value, gain_query, gain_key)
    own_pair, outer_latents = lax.optimization_barrier((own_pair, outer_latents))
    inner_pair = lax.ppermute(own_pair, "ctx", [(i, i ^ 1) for i in range(count)])
    outer_pair = call(
        functools.partial(project_kernel, False, block, chunk),
        struct((rows, 2 * width), BF16),
        [VMEM, VMEM] + [ANY] * 4 + [VMEM],
        scratch,
        flops=flops,
        moved=4 * MIB,
    )(outer_latents, features, w_embed, w_time, w_key[0], w_value[0], gain_key)
    sent = call(
        attend_kernel,
        struct(packed, BF16),
        [SMEM] + [VMEM] * 10,
        flops=flops // 8,
        moved=4 * MIB,
    )(
        plan,
        query,
        own_pair,
        inner_pair,
        outer_pair,
        tail,
        latents,
        features,
        into_final,
        state,
        noise,
    )
    taken = lax.all_to_all(sent, "tm", 0, 0, tiled=True)
    total = call(sum_kernel, struct((channels, tile), F32), [VMEM], limit=8)(taken)
    return total.T[None]


def solution(mesh):
    return jax.shard_map(
        per_device,
        mesh=mesh,
        in_specs=(
            P("tm", "ctx", None),
            P("tm", "ctx", None),
            P(),
            P(),
            P(),
            P("tm", None, None),
            P("tm", None, None),
            P("tm", None, None),
            P("tm", None),
            P("tm", None),
            P("tm", None, None),
            P(),
        ),
        out_specs=P("tm", "ctx", None),
        check_vma=False,
    )
```

time: 258 us -> 72.5 us (0.28)
  the two profiles are of different devices: /device:TPU:8 before, /device:TPU:24 now
where the time goes in v1:
time: 72.5 us; the launch traced here: 72 us
  Pallas kernels  26.6 us (37%)
  starting transfers between devices  20.8 us (29%)
  blocking collectives  14.4 us (20%)
  local copies, waits for them, and re-layouts  6.49 us (9%)
  waiting for transfers between devices  3.3 us (5%)
    all_to_all x1, blocking collectives, per_device(): taken = lax.all_to_all(sent, 'tm', 0, 0, tiled=True)  14.4 us
    pallas_call x1, Pallas kernels, per_device(): call(attend_kernel, struct(packed, BF16), [SMEM] + [VMEM] * 10, flops=flo...  8.8 us
    all_to_all x1, starting transfers between devices, per_device(): latents = lax.all_to_all(copies, 'tm', 0, 0, tiled=True)  8.47 us
    ppermute x1, starting transfers between devices, per_device(): outer_latents = lax.ppermute(latents, 'ctx', outward)  8.16 us
    pallas_call x1, Pallas kernels, per_device(): call(functools.partial(project_kernel, True, block, chunk), [struct((rows...  7.66 us
    pallas_call x1, Pallas kernels, per_device(): call(functools.partial(project_kernel, False, block, chunk), struct((rows...  7.44 us
    unnamed x32, local copies, waits for them, and re-layouts  6.49 us
    ppermute x1, starting transfers between devices, per_device(): lax.ppermute(own_pair, 'ctx', [(i, i ^ 1) for i in range(count)])  4.22 us
  transfers between devices with their start and end apart: 3, of which 1 were waited for; matrix products, arithmetic and copies ran while one was open for 0% of the time, Pallas kernels for 22%

profile of v1, /device:TPU:24, one launch (start us, length us, event | category | flops | bytes accessed | tf_op | source)
XLA Modules:
  0.0 72.0 jit_solution(2965472797662687866)
XLA Ops:
  0.0 0.0 copy-start.5
  0.0 0.0 copy-start.8
  0.0 0.8 %copy-done.8 = f32[1,96,64]{1,2,0:T(8,128)S(1)} copy-done((f32[1,96,64]{1,2,0:T(8,128)S(1)}, f32[1,96,64]{1,2,0:T(8,128)}, u32[]{:S(2)}) %copy-start.8) | copy-done | bytes 24600
  0.8 0.8 %shard_map.118 = bf16[16,48,128]{2,1,0:T(8,128)(2,1)} custom-call(f32[64,96]{1,0:T(8,128)S(1)} %bitcast.18), custom_call_target="tpu_custom_call" | custom-call | tf_op jit(solution)/shard_map/pallas_call | solution.py:230
  1.7 8.5 %all-to-all-start = ((bf16[16,48,128]{2,1,0:T(8,128)(2,1)}), bf16[16,48,128]{2,1,0:T(8,128)(2,1)S(1)}, u32[]{:S(2)}, u32[]{:S(2)}) async-start(bf16[16,48,128]{2,1,0:T(8,128)(2,1)} %shard_map.118), calls=%async_computation | async-start | bytes 393216 | tf_op jit(solution)/shard_map/all_to_all | solution.py:231
  10.1 0.0 copy-done.5
  10.1 0.0 copy-start
  10.2 1.1 %copy-done = bf16[1,128,3072]{2,1,0:T(8,128)(2,1)S(1)} copy-done((bf16[1,128,3072]{2,1,0:T(8,128)(2,1)S(1)}, bf16[1,128,3072]{2,1,0:T(8,128)(2,1)}, u32[]{:S(2)}) %copy-start) | copy-done | bytes 786456
  11.3 0.0 copy-start.1
  11.3 1.1 %copy-done.1 = bf16[128,3072]{1,0:T(8,128)(2,1)S(1)} copy-done((bf16[128,3072]{1,0:T(8,128)(2,1)S(1)}, bf16[128,3072]{1,0:T(8,128)(2,1)}, u32[]{:S(2)}) %copy-start.1) | copy-done | bytes 786456
  12.4 0.0 copy-start.3
  12.4 1.1 %copy-done.3 = bf16[1,3072,128]{2,1,0:T(8,128)(2,1)S(1)} copy-done((bf16[1,3072,128]{2,1,0:T(8,128)(2,1)S(1)}, bf16[1,3072,128]{2,1,0:T(8,128)(2,1)}, u32[]{:S(2)}) %copy-start.3) | copy-done | bytes 786456
  13.5 0.0 copy-start.6
  13.6 1.0 %copy-done.6 = bf16[64,3072]{1,0:T(8,128)(2,1)S(1)} copy-done((bf16[64,3072]{1,0:T(8,128)(2,1)S(1)}, bf16[64,3072]{1,0:T(8,128)(2,1)}, u32[]{:S(2)}) %copy-start.6) | copy-done | bytes 393240
  14.5 0.0 copy-start.2
  14.5 0.0 copy-start.7
  14.6 0.0 copy-start.12
  14.6 0.0 copy-start.13
  14.6 1.0 %shard_map.119 = (bf16[192,256]{1,0:T(8,128)(2,1)S(1)}, bf16[192,128]{1,0:T(8,128)(2,1)S(1)}, bf16[128,128]{1,0:T(8,128)(2,1)S(1)}) custom-call(bf16[64,3072]{1,0:T(8,128)(2,1)S(1)} %copy-done.6, bf16[128,3072]{1,0:T(8,128)(2,1)S(1)} %copy-done.1, bf16[3072,128]{1,0:T(8,128)(2,1)S(1)} %bitcast.15, bf16[128,3072]{1,0:T(8,128)(2,1)S(1)} %bitcast.14, ...), custom_call_target="tpu_custom_call" | custom-call | tf_op jit(solution)/shard_map/pallas_call | solution.py:234
  15.6 0.0 copy-start.11
  15.6 0.6 copy-done.11
  16.3 0.1 fusion
  16.4 0.1 pad_maximum_fusion.feature_ref
  16.5 3.3 %all-to-all-done.latent_ref = bf16[16,48,128]{2,1,0:T(8,128)(2,1)S(1)} async-done(((bf16[16,48,128]{2,1,0:T(8,128)(2,1)}), bf16[16,48,128]{2,1,0:T(8,128)(2,1)S(1)}, u32[]{:S(2)}, u32[]{:S(2)}) %all-to-all-start) | async-done | bytes 196640 | tf_op jit(solution)/shard_map/all_to_all | solution.py:231
  19.8 8.2 %collective-permute-start = (bf16[16,48,128]{2,1,0:T(8,128)(2,1)S(1)}, bf16[16,48,128]{2,1,0:T(8,128)(2,1)S(1)}, u32[]{:S(2)}, u32[]{:S(2)}) collective-permute-start(bf16[16,48,128]{2,1,0:T(8,128)(2,1)S(1)} %all-to-all-done.latent_ref), channel_id=1, source_target_pairs={{1,2},{2,1},{3,4},{4,3},{5,6},{6,5},{7,8},{8,7},{9,10},{10,9},{11,... | collective-permute-start | bytes 589832 | tf_op jit(solution)/shard_map/ppermute | solution.py:233
  27.9 0.0 copy-start.14
  27.9 0.0 copy-start.15
  28.0 0.0 copy-done.2
  28.0 0.0 copy-done.7
  28.0 0.0 copy-done.12
  28.0 0.0 copy-done.13
  28.0 0.6 copy-done.14
  28.6 0.0 copy-done.15
  28.6 0.0 copy-start.4
  28.6 7.7 %shard_map.120 = (bf16[1536,128]{1,0:T(8,128)(2,1)S(1)}, bf16[1536,256]{1,0:T(8,128)(2,1)S(1)}) custom-call(bf16[16,48,128]{2,1,0:T(8,128)(2,1)S(1)} %all-to-all-done.latent_ref, bf16[16,128]{1,0:T(8,128)(2,1)S(1)} %pad_maximum_fusion.feature_ref, bf16[64,3072]{1,0:T(8,128)(2,1)S(1)} %copy-done.7, bf16[128,3072]{1,0:T(8,128)(2,1)S(1)} %copy-done.2, ...), custom_call_target="tpu_custom_call" | custom-call | flops 4831838208 | bytes 4194304 | tf_op jit(solution)/shard_map/pallas_call | solution.py:251
  36.3 0.0 collective-permute-done.latent_ref
  36.3 0.0 copy-start.9
  36.3 0.0 copy-start.10
  36.3 4.2 %collective-permute-start.1 = (bf16[1536,256]{1,0:T(8,128)(2,1)S(1)}, bf16[1536,256]{1,0:T(8,128)(2,1)S(1)}, u32[]{:S(2)}, u32[]{:S(2)}) collective-permute-start(bf16[1536,256]{1,0:T(8,128)(2,1)S(1)} %get-tuple-element.15.own_ref), channel_id=1, source_target_pairs={{0,1},{1,0},{2,3},{3,2},{4,5},{5,4},{6,7},{7,6},{8,9},{9,8},{10,11... | collective-permute-start | bytes 2359304 | tf_op jit(solution)/shard_map/ppermute | solution.py:260
  40.5 0.0 copy-done.4
  40.5 7.4 %shard_map.121.outer_ref = bf16[1536,256]{1,0:T(8,128)(2,1)S(1)} custom-call(bf16[16,48,128]{2,1,0:T(8,128)(2,1)S(1)} %collective-permute-done.latent_ref, bf16[16,128]{1,0:T(8,128)(2,1)S(1)} %pad_maximum_fusion.feature_ref, bf16[64,3072]{1,0:T(8,128)(2,1)S(1)} %copy-done.7, bf16[128,3072]{1,0:T(8,128)(2,1)S(1)} %copy-done.2, ...), custom_call_target="tpu_custom_call" | custom-call | flops 4831838208 | bytes 4194304 | tf_op jit(solution)/shard_map/pallas_call | solution.py:261
  48.0 0.0 collective-permute-done.1.inner_ref
  48.0 0.0 copy-done.9
  48.0 0.0 copy-done.10
  48.0 8.8 %shard_map.122 = bf16[16,48,128]{2,1,0:T(8,128)(2,1)S(1)} custom-call(s32[17]{0:T(128)S(1)} %copy-done.11, bf16[1536,128]{1,0:T(8,128)(2,1)S(1)} %get-tuple-element.13.query_ref, bf16[1536,256]{1,0:T(8,128)(2,1)S(1)} %get-tuple-element.15.own_ref, bf16[1536,256]{1,0:T(8,128)(2,1)S(1)} %collective-permute-done.1.inner_ref, ...), custom_call_target="tpu_custom_call" | custom-call | flops 603979776 | bytes 4194304 | tf_op jit(solution)/shard_map/pallas_call | solution.py:269
  56.8 14.4 %all_to_all.10.taken_ref = bf16[16,48,128]{2,1,0:T(8,128)(2,1)S(1)} all-to-all(bf16[16,48,128]{2,1,0:T(8,128)(2,1)S(1)} %shard_map.122), channel_id=1, replica_groups=mesh['tm'=16,'ctx'=32] {'tm'}, dimensions={0} | all-to-all | bytes 393216 | tf_op jit(solution)/shard_map/all_to_all | solution.py:288
  71.3 0.8 %shard_map.123 = f32[64,96]{1,0:T(8,128)} custom-call(bf16[16,48,128]{2,1,0:T(8,128)(2,1)S(1)} %all_to_all.10.taken_ref), custom_call_target="tpu_custom_call" | custom-call | tf_op jit(solution)/shard_map/pallas_call | solution.py:289
  (2 shorter events, 0.0 us)
Async XLA Ops:
  0.0 10.1 %copy-start.5 = (bf16[3072,64]{0,1:T(8,128)(2,1)S(1)}, bf16[3072,64]{0,1:T(8,128)(2,1)}, u32[]{:S(2)}) copy-start(bf16[3072,64]{0,1:T(8,128)(2,1)} %param.23) | copy-start | bytes 1179652
  0.0 0.8 %copy-start.8 = (f32[1,96,64]{1,2,0:T(8,128)S(1)}, f32[1,96,64]{1,2,0:T(8,128)}, u32[]{:S(2)}) copy-start(f32[1,96,64]{1,2,0:T(8,128)} %param.12) | copy-start | bytes 73732
  1.7 18.1 %all-to-all-start = ((bf16[16,48,128]{2,1,0:T(8,128)(2,1)}), bf16[16,48,128]{2,1,0:T(8,128)(2,1)S(1)}, u32[]{:S(2)}, u32[]{:S(2)}) async-start(bf16[16,48,128]{2,1,0:T(8,128)(2,1)} %shard_map.118), calls=%async_computation | async-start | bytes 393216 | tf_op jit(solution)/shard_map/all_to_all | solution.py:231
  10.1 1.1 %copy-start = (bf16[1,128,3072]{2,1,0:T(8,128)(2,1)S(1)}, bf16[1,128,3072]{2,1,0:T(8,128)(2,1)}, u32[]{:S(2)}) copy-start(bf16[1,128,3072]{2,1,0:T(8,128)(2,1)} %param.22) | copy-start | bytes 2359300
  11.3 1.1 %copy-start.1 = (bf16[128,3072]{1,0:T(8,128)(2,1)S(1)}, bf16[128,3072]{1,0:T(8,128)(2,1)}, u32[]{:S(2)}) copy-start(bf16[128,3072]{1,0:T(8,128)(2,1)} %time_ref.5) | copy-start | bytes 2359300
  12.4 1.1 %copy-start.3 = (bf16[1,3072,128]{2,1,0:T(8,128)(2,1)S(1)}, bf16[1,3072,128]{2,1,0:T(8,128)(2,1)}, u32[]{:S(2)}) copy-start(bf16[1,3072,128]{2,1,0:T(8,128)(2,1)} %param.19) | copy-start | bytes 2359300
  13.5 1.0 %copy-start.6 = (bf16[64,3072]{1,0:T(8,128)(2,1)S(1)}, bf16[64,3072]{1,0:T(8,128)(2,1)}, u32[]{:S(2)}) copy-start(bf16[64,3072]{1,0:T(8,128)(2,1)} %embed_ref.5) | copy-start | bytes 1179652
  14.5 13.4 %copy-start.2 = (bf16[128,3072]{1,0:T(8,128)(2,1)S(1)}, bf16[128,3072]{1,0:T(8,128)(2,1)}, u32[]{:S(2)}) copy-start(bf16[128,3072]{1,0:T(8,128)(2,1)} %time_ref.5) | copy-start | bytes 2359300
  14.5 13.4 %copy-start.7 = (bf16[64,3072]{1,0:T(8,128)(2,1)S(1)}, bf16[64,3072]{1,0:T(8,128)(2,1)}, u32[]{:S(2)}) copy-start(bf16[64,3072]{1,0:T(8,128)(2,1)} %embed_ref.5) | copy-start | bytes 1179652
  14.6 13.4 %copy-start.12 = (bf16[1,3072,128]{2,1,0:T(8,128)(2,1)S(1)}, bf16[1,3072,128]{2,1,0:T(8,128)(2,1)}, u32[]{:S(2)}) copy-start(bf16[1,3072,128]{2,1,0:T(8,128)(2,1)} %param.17) | copy-start | bytes 2359300
  14.6 13.4 %copy-start.13 = (bf16[1,3072,128]{2,1,0:T(8,128)(2,1)S(1)}, bf16[1,3072,128]{2,1,0:T(8,128)(2,1)}, u32[]{:S(2)}) copy-start(bf16[1,3072,128]{2,1,0:T(8,128)(2,1)} %param.18) | copy-start | bytes 2359300
  15.6 0.7 copy-start.11
  19.8 16.5 %collective-permute-start = (bf16[16,48,128]{2,1,0:T(8,128)(2,1)S(1)}, bf16[16,48,128]{2,1,0:T(8,128)(2,1)S(1)}, u32[]{:S(2)}, u32[]{:S(2)}) collective-permute-start(bf16[16,48,128]{2,1,0:T(8,128)(2,1)S(1)} %all-to-all-done.latent_ref), channel_id=1, source_target_pairs={{1,2},{2,1},{3,4},{4,3},{5,6},{6,5},{7,8},{8,7},{9,10},{10,9},{11,... | collective-permute-start | bytes 589832 | tf_op jit(solution)/shard_map/ppermute | solution.py:233
  27.9 0.7 copy-start.14
  27.9 0.7 copy-start.15
  28.6 11.9 %copy-start.4 = (bf16[1,3072,128]{2,1,0:T(8,128)(2,1)S(1)}, bf16[1,3072,128]{2,1,0:T(8,128)(2,1)}, u32[]{:S(2)}) copy-start(bf16[1,3072,128]{2,1,0:T(8,128)(2,1)} %param.19) | copy-start | bytes 2359300
  36.3 11.7 %copy-start.9 = (f32[1,96,64]{1,2,0:T(8,128)S(1)}, f32[1,96,64]{1,2,0:T(8,128)}, u32[]{:S(2)}) copy-start(f32[1,96,64]{1,2,0:T(8,128)} %param.12) | copy-start | bytes 73732
  36.3 11.7 %copy-start.10 = (f32[1,96,64]{1,2,0:T(8,128)S(1)}, f32[1,96,64]{1,2,0:T(8,128)}, u32[]{:S(2)}) copy-start(f32[1,96,64]{1,2,0:T(8,128)} %param.13) | copy-start | bytes 73732
  36.3 11.7 %collective-permute-start.1 = (bf16[1536,256]{1,0:T(8,128)(2,1)S(1)}, bf16[1536,256]{1,0:T(8,128)(2,1)S(1)}, u32[]{:S(2)}, u32[]{:S(2)}) collective-permute-start(bf16[1536,256]{1,0:T(8,128)(2,1)S(1)} %get-tuple-element.15.own_ref), channel_id=1, source_target_pairs={{0,1},{1,0},{2,3},{3,2},{4,5},{5,4},{6,7},{7,6},{8,9},{9,8},{10,11... | collective-permute-start | bytes 2359304 | tf_op jit(solution)/shard_map/ppermute | solution.py:260

commit v2 on v1

v2 whole, which is shorter than its diff:
```python
import functools
import math

import jax
import jax.numpy as jnp
from jax import lax
from jax.experimental import pallas as pl
from jax.experimental.pallas import tpu as pltpu
from jax.sharding import PartitionSpec as P

F32, BF16 = jnp.float32, jnp.bfloat16
MIB = 1 << 20
FOLD_LIMIT = 54
VMEM = pl.BlockSpec(memory_space=pltpu.VMEM)
HBM = pl.BlockSpec(memory_space=pltpu.HBM)
SMEM = pl.BlockSpec(memory_space=pltpu.SMEM)
NT = (((1,), (1,)), ((), ()))


def fourier_rows(plan, freq_count, step_count):
    half_freq = freq_count // 2
    frequency = jnp.exp(-math.log(10000.0) * jnp.arange(half_freq, dtype=F32) / half_freq)
    phase_arg = plan[:step_count].astype(F32)[:, None] * frequency[None, :]
    return jnp.concatenate([jnp.cos(phase_arg), jnp.sin(phase_arg)], axis=1).astype(BF16)


def dot(a, b):
    return jnp.dot(a, b, preferred_element_type=F32)


def split(value):
    high = value.astype(BF16)
    return high, (value - high.astype(F32)).astype(BF16)


def pack_kernel(state_ref, own_ref, copies_ref):
    rows = state_ref[...].T.astype(BF16)
    half = rows.shape[0] // 2
    packed = jnp.concatenate([rows[:half], rows[half:]], axis=1)
    own_ref[...] = packed
    copies_ref[...] = jnp.broadcast_to(packed[None], copies_ref.shape)


def input_rows(packed, features):
    low = lax.broadcasted_iota(jnp.int32, packed.shape, 1) < packed.shape[1] // 2
    zero = jnp.zeros_like(packed)
    rows = jnp.concatenate([jnp.where(low, packed, zero), jnp.where(low, zero, packed)], axis=0)
    features = jnp.broadcast_to(features, (rows.shape[0], features.shape[1]))
    return jnp.concatenate([features, rows], axis=1)


def fold_kernel(
    plan_ref,
    own_ref,
    feature_ref,
    state_ref,
    noise_ref,
    embed_hbm,
    time_hbm,
    value_hbm,
    out_hbm,
    final_hbm,
    gain_query_hbm,
    gain_key_hbm,
    into_value,
    tail,
    extra_ref,
    gains,
    sizes,
    first,
    value_ref,
    out_ref,
    final_ref,
    sems,
):
    freq, width = time_hbm.shape[0], value_hbm.shape[1]
    channels = embed_hbm.shape[0]
    pairs = (
        (time_hbm, first.at[:freq]),
        (embed_hbm, first.at[freq:]),
        (value_hbm, value_ref),
        (final_hbm, final_ref),
        (out_hbm, out_ref),
        (gain_query_hbm, gains.at[0:1]),
        (gain_key_hbm, gains.at[1:2]),
    )
    copies = [pltpu.make_async_copy(a, b, sems.at[i]) for i, (a, b) in enumerate(pairs)]
    for copy in copies:
        copy.start()
    mine = lax.axis_index("tm")
    features = feature_ref[...].astype(F32)
    chosen = lax.broadcasted_iota(jnp.int32, features.shape, 0) == mine
    features = jnp.sum(jnp.where(chosen, features, 0.0), axis=0, keepdims=True).astype(BF16)
    taken = input_rows(own_ref[...], features)
    for s in range(sizes.shape[0]):
        size = (plan_ref[s] - plan_ref[s + 1]).astype(F32) / 1000.0
        sizes[s : s + 1, :] = jnp.full((1, sizes.shape[1]), size, F32)
    size = (plan_ref[mine] - plan_ref[mine + 1]).astype(F32) / 1000.0
    size = jnp.full((taken.shape[0], channels), size, F32)
    for copy in copies:
        copy.wait()
    left, final = first[...], final_ref[...]
    high, low = split(dot(left, value_ref[...]))
    into_value[:, :width] = jnp.concatenate([high, high[freq:]], axis=0)
    into_value[:, width:] = jnp.concatenate([low, low[freq:]], axis=0)
    product = lax.dot_general(left, final, NT, preferred_element_type=F32)
    product = jnp.concatenate(split(product), axis=1)
    residual = dot(taken, jnp.concatenate([product, product[freq:]], axis=0))
    residual = residual[:, :channels] + residual[:, channels:]
    state = state_ref[...].T
    rest = state - state.astype(BF16).astype(F32)
    extra = size * residual + jnp.sqrt(size) * noise_ref[...].T + jnp.where(mine == 0, rest, 0.0)
    half = extra.shape[0] // 2
    extra_ref[...] = jnp.concatenate([extra[:half], extra[half:]], axis=1)
    high, low = split(lax.dot_general(out_ref[...], final, NT, preferred_element_type=F32))
    tail[:width, :] = jnp.concatenate([high, high], axis=1)
    tail[width:, :] = jnp.concatenate([low, low], axis=1)


def rms_gain(values, gain):
    scale = lax.rsqrt(jnp.mean(values * values, axis=-1, keepdims=True) + 1e-06)
    return values * scale * gain


def project_kernel(
    own, group, chunk, latent_ref, feature_ref, time_ref, embed_ref, left_ref, right_ref, gains, *rest
):
    if own:
        into_value, query_out, pair_out = rest
    else:
        (pair_out,) = rest
    steps, half, _ = latent_ref.shape
    depth, width = left_ref.shape
    tile = 2 * half
    features = feature_ref[...].astype(F32)
    for s in range(0, steps, group):
        here = slice(s * tile, (s + group) * tile)
        taken = [
            input_rows(latent_ref[t], features[t : t + 1].astype(BF16)) for t in range(s, s + group)
        ]
        taken = jnp.concatenate(taken, axis=0)
        total = None
        for n in range(0, depth, chunk):
            part = slice(n, n + chunk)
            embed = embed_ref[:, part]
            first = jnp.concatenate([time_ref[:, part], embed, embed], axis=0)
            second = jnp.concatenate([left_ref[part, :], right_ref[part, :]], axis=1)
            product = dot(dot(taken, first).astype(BF16), second)
            total = product if total is None else total + product
        if own:
            query_out[here, :] = rms_gain(total[:, :width], gains[0:1, :]).astype(BF16)
            pair_out[here, :width] = rms_gain(total[:, width:], gains[1:2, :]).astype(BF16)
            values = dot(taken, into_value[...])
            pair_out[here, width:] = (values[:, :width] + values[:, width:]).astype(BF16)
        else:
            pair_out[here, :width] = rms_gain(total[:, :width], gains[1:2, :]).astype(BF16)
            pair_out[here, width:] = total[:, width:].astype(BF16)


def attend_kernel(
    group, query_ref, own_ref, inner_ref, outer_ref, tail_ref, extra_ref, sizes, sent_ref, scores
):
    steps, half, both = sent_ref.shape
    tile, width = 2 * half, query_ref.shape[1]
    pairs = (own_ref, inner_ref, outer_ref)
    mine, place = lax.axis_index("tm"), lax.axis_index("ctx")
    rate = math.log2(math.e) / math.sqrt(width)
    for s in range(steps):
        here = slice(s * tile, (s + 1) * tile)
        keys = jnp.concatenate([r[here, :width] for r in pairs], axis=0)
        scores[here, :] = lax.dot_general(query_ref[here, :], keys, NT, preferred_element_type=F32)

    @pl.when((place == 0) | (place == lax.axis_size("ctx") - 1))
    def _():
        scores[:, 2 * tile :] = jnp.full((steps * tile, tile), -1e30, F32)

    low = lax.broadcasted_iota(jnp.int32, (half, both), 1) < both // 2
    running, extra = jnp.zeros((half, both), F32), extra_ref[...]
    for s in range(0, steps, group):
        values = scores[s * tile : (s + group) * tile, :]
        top = jnp.max(values, axis=-1, keepdims=True)
        expo = jnp.exp2((values - top) * rate)
        probs = (expo * (1.0 / jnp.sum(expo, axis=-1, keepdims=True))).astype(BF16)
        attended = []
        for t in range(s, s + group):
            here = slice(t * tile, (t + 1) * tile)
            seen = jnp.concatenate([r[here, width:] for r in pairs], axis=0)
            attended.append(dot(probs[(t - s) * tile : (t - s + 1) * tile], seen).astype(BF16))
        attended = jnp.concatenate(attended, axis=0)
        terms = dot(jnp.concatenate([attended, attended], axis=1), tail_ref[...])
        for t in range(s, s + group):
            row = (t - s) * tile
            packed = jnp.where(low, terms[row : row + half], terms[row + half : row + tile])
            running = running + sizes[t : t + 1, :] * packed
            sent_ref[t] = (running + jnp.where(t >= mine, extra, 0.0)).astype(BF16)


def sum_kernel(taken_ref, latent_ref, out_ref):
    total = jnp.sum(taken_ref[...].astype(F32), axis=0) + latent_ref[0].astype(F32)
    channels = total.shape[1] // 2
    out_ref[...] = jnp.concatenate([total[:, :channels], total[:, channels:]], axis=0).T


def call(kernel, shapes, specs, scratch=(), limit=24, flops=0, moved=0):
    many = isinstance(shapes, (list, tuple))
    return pl.pallas_call(
        kernel,
        out_shape=shapes,
        in_specs=specs,
        out_specs=[VMEM] * len(shapes) if many else VMEM,
        scratch_shapes=list(scratch),
        compiler_params=pltpu.CompilerParams(vmem_limit_bytes=limit * MIB),
        cost_estimate=pl.CostEstimate(flops=flops, bytes_accessed=moved, transcendentals=0),
    )


def struct(shape, dtype):
    return jax.ShapeDtypeStruct(shape, dtype)


def per_device(
    states,
    noise_draws,
    plan,
    w_embed,
    w_time,
    w_query,
    w_key,
    w_value,
    gain_query,
    gain_key,
    w_out,
    w_final,
):
    steps = lax.axis_size("tm")
    tile, channels = states.shape[1:]
    freq, depth = w_time.shape
    width = w_query.shape[2]
    count = lax.axis_size("ctx")
    rows = steps * tile
    state, noise = states[0].T, noise_draws[0].T
    final = w_final.T
    packed = (steps, tile // 2, 2 * channels)
    features = fourier_rows(plan, freq, steps)

    own, copies = call(
        pack_kernel, [struct(packed[1:], BF16), struct(packed, BF16)], [VMEM], limit=8
    )(state)
    latents = lax.all_to_all(copies, "tm", 0, 0, tiled=True)
    outward = [(i, i + 1 if i % 2 else i - 1) for i in range(1, count - 1)]
    outer_latents = lax.ppermute(latents, "ctx", outward)
    inputs = freq + 2 * channels
    into_value, tail, extra, gains, sizes = call(
        fold_kernel,
        [
            struct((inputs, 2 * width), BF16),
            struct((2 * width, 2 * channels), BF16),
            struct(packed[1:], F32),
            struct((2, width), F32),
            struct((steps, 2 * channels), F32),
        ],
        [SMEM] + [VMEM] * 4 + [HBM] * 7,
        [
            pltpu.VMEM((freq + channels, depth), BF16),
            pltpu.VMEM((depth, width), BF16),
            pltpu.VMEM((width, depth), BF16),
            pltpu.VMEM((channels, depth), BF16),
            pltpu.SemaphoreType.DMA((7,)),
        ],
        limit=FOLD_LIMIT,
        flops=MIB,
        moved=1024,
    )(
        plan,
        own,
        features,
        state,
        noise,
        w_embed,
        w_time,
        w_value[0],
        w_out[0],
        final,
        gain_query,
        gain_key,
    )
    flops = 40 * rows * depth * 256
    query, own_pair = call(
        functools.partial(project_kernel, True, 4, 256),
        [struct((rows, width), BF16), struct((rows, 2 * width), BF16)],
        [VMEM] * 8,
        flops=flops,
        moved=4 * MIB,
    )(latents, features, w_time, w_embed, w_query[0], w_key[0], gains, into_value)
    inner_pair = lax.ppermute(own_pair, "ctx", [(i, i ^ 1) for i in range(count)])
    outer_pair = call(
        functools.partial(project_kernel, False, 4, 256),
        struct((rows, 2 * width), BF16),
        [VMEM] * 7,
        flops=flops,
        moved=4 * MIB,
    )(outer_latents, features, w_time, w_embed, w_key[0], w_value[0], gains)
    sent = call(
        functools.partial(attend_kernel, 4),
        struct(packed, BF16),
        [VMEM] * 7,
        [pltpu.VMEM((rows, 3 * tile), F32)],
        flops=flops // 8,
        moved=4 * MIB,
    )(query, own_pair, inner_pair, outer_pair, tail, extra, sizes)
    taken = lax.all_to_all(sent, "tm", 0, 0, tiled=True)
    total = call(sum_kernel, struct((channels, tile), F32), [VMEM] * 2, limit=8)(taken, latents)
    return total.T[None]


def solution(mesh):
    return jax.shard_map(
        per_device,
        mesh=mesh,
        in_specs=(
            P("tm", "ctx", None),
            P("tm", "ctx", None),
            P(),
            P(),
            P(),
            P("tm", None, None),
            P("tm", None, None),
            P("tm", None, None),
            P("tm", None),
            P("tm", None),
            P("tm", None, None),
            P(),
        ),
        out_specs=P("tm", "ctx", None),
        check_vma=False,
    )
```

time: 72.5 us -> 62.5 us (0.86)
  Pallas kernels: 26.6 us -> 20.2 us
  local copies, waits for them, and re-layouts: 6.49 us -> 3.54 us
  starting transfers between devices: 20.8 us -> 19.9 us
    pallas_call x6, Pallas kernels: 26.6 us -> 20.2 us  [the longest x1 5.71 us: per_device(): call(functools.partial(project_kernel, True, 4, 256), [struct((rows, widt...]
    unnamed x32 -> x28, local copies, waits for them, and re-layouts: 6.49 us -> 3.54 us
    ppermute x1, starting transfers between devices: 4.22 us -> 3.25 us  [per_device(): lax.ppermute(own_pair, 'ctx', [(i, i ^ 1) for i in range(count)])]
  transfers between devices with their start and end apart: 3 -> 3, of which waited for: 1 -> 1; matrix products, arithmetic and copies ran while one was open for 0% -> 1% of each run, Pallas kernels for 22% -> 26%
where the time goes in v2:
time: 62.5 us; the launch traced here: 62.1 us
  Pallas kernels  20.2 us (32%)
  starting transfers between devices  19.9 us (32%)
  blocking collectives  14.6 us (23%)
  local copies, waits for them, and re-layouts  3.54 us (6%)
  waiting for transfers between devices  2.96 us (5%)
  other arithmetic  0.8 us (1%)
    all_to_all x1, blocking collectives, per_device(): taken = lax.all_to_all(sent, 'tm', 0, 0, tiled=True)  14.6 us
    all_to_all x1, starting transfers between devices, per_device(): latents = lax.all_to_all(copies, 'tm', 0, 0, tiled=True)  8.47 us
    ppermute x1, starting transfers between devices, per_device(): outer_latents = lax.ppermute(latents, 'ctx', outward)  8.16 us
    pallas_call x1, Pallas kernels, per_device(): call(functools.partial(project_kernel, True, 4, 256), [struct((rows, widt...  5.71 us
    pallas_call x1, Pallas kernels, per_device(): call(functools.partial(project_kernel, False, 4, 256), struct((rows, 2 *...  5.39 us
    pallas_call x1, Pallas kernels, per_device(): call(fold_kernel, [struct((inputs, 2 * width), BF16), struct((2 * width,...  5.18 us
    unnamed x28, local copies, waits for them, and re-layouts  3.54 us
    ppermute x1, starting transfers between devices, per_device(): lax.ppermute(own_pair, 'ctx', [(i, i ^ 1) for i in range(count)])  3.25 us
  transfers between devices with their start and end apart: 3, of which 1 were waited for; matrix products, arithmetic and copies ran while one was open for 1% of the time, Pallas kernels for 26%

profile of v2, /device:TPU:24, one launch (start us, length us, event | category | flops | bytes accessed | tf_op | source)
XLA Modules:
  0.0 62.1 jit_solution(8978253642495660399)
XLA Ops:
  0.0 0.0 copy-start.3
  0.0 0.8 %copy-done.3 = f32[1,96,64]{1,2,0:T(8,128)S(1)} copy-done((f32[1,96,64]{1,2,0:T(8,128)S(1)}, f32[1,96,64]{1,2,0:T(8,128)}, u32[]{:S(2)}) %copy-start.3) | copy-done | bytes 24600
  0.8 0.8 %shard_map.118 = (bf16[48,128]{1,0:T(8,128)(2,1)S(1)}, bf16[16,48,128]{2,1,0:T(8,128)(2,1)}) custom-call(f32[64,96]{1,0:T(8,128)S(1)} %bitcast.17), custom_call_target="tpu_custom_call" | custom-call | tf_op jit(solution)/shard_map/pallas_call | solution.py:246
  1.6 0.0 copy-start.5
  1.6 0.6 copy-done.5
  2.2 8.5 %all-to-all-start = ((bf16[16,48,128]{2,1,0:T(8,128)(2,1)}), bf16[16,48,128]{2,1,0:T(8,128)(2,1)S(1)}, u32[]{:S(2)}, u32[]{:S(2)}) async-start(bf16[16,48,128]{2,1,0:T(8,128)(2,1)} %get-tuple-element.14), calls=%async_computation | async-start | bytes 393216 | tf_op jit(solution)/shard_map/all_to_all | solution.py:249
  10.7 0.0 copy-start.13
  10.7 0.6 %copy-done.13 = s32[17]{0:T(128)S(1)} copy-done((s32[17]{0:T(128)S(1)}, s32[17]{0:T(128)}, u32[]{:S(2)}) %copy-start.13) | copy-done | bytes 92
  11.3 0.1 fusion
  11.5 0.7 %pad_maximum_fusion.feature_ref = bf16[16,128]{1,0:T(8,128)(2,1)} fusion(bf16[16,64]{1,0:T(8,128)(2,1)S(1)} %get-tuple-element.24, bf16[16,64]{1,0:T(8,128)(2,1)S(1)} %get-tuple-element.23), kind=kLoop, calls=%fused_computation.4 | loop fusion | flops 8192 | bytes 8192 | tf_op jit(solution)/shard_map/concatenate | solution.py:24
  12.1 0.0 copy-start
  12.1 0.0 copy-start.2
  12.1 0.0 copy-start.6
  12.1 0.0 copy-start.7
  12.1 5.2 %shard_map.119 = (bf16[256,256]{1,0:T(8,128)(2,1)}, bf16[256,128]{1,0:T(8,128)(2,1)}, f32[48,128]{1,0:T(8,128)}, f32[2,128]{1,0:T(2,128)}, f32[16,128]{1,0:T(8,128)}) custom-call(s32[17]{0:T(128)} %plan_ref.1, bf16[48,128]{1,0:T(8,128)(2,1)} %copy-done.5, bf16[16,128]{1,0:T(8,128)(2,1)} %pad_maximum_fusion.feature_ref, f32[64,96]{1,0:T(8,128)} %bitcast.16, ...), custom_call_target="tpu_custom_call" | custom-call | flops 1048576 | bytes 1024 | tf_op jit(solution)/shard_map/pallas_call | solution.py:253
  17.3 0.0 copy-start.4
  17.3 3.0 %all-to-all-done.latent_ref = bf16[16,48,128]{2,1,0:T(8,128)(2,1)S(1)} async-done(((bf16[16,48,128]{2,1,0:T(8,128)(2,1)}), bf16[16,48,128]{2,1,0:T(8,128)(2,1)S(1)}, u32[]{:S(2)}, u32[]{:S(2)}) %all-to-all-start) | async-done | bytes 196640 | tf_op jit(solution)/shard_map/all_to_all | solution.py:249
  20.3 8.2 %collective-permute-start.1 = (bf16[16,48,128]{2,1,0:T(8,128)(2,1)S(1)}, bf16[16,48,128]{2,1,0:T(8,128)(2,1)S(1)}, u32[]{:S(2)}, u32[]{:S(2)}) collective-permute-start(bf16[16,48,128]{2,1,0:T(8,128)(2,1)S(1)} %all-to-all-done.latent_ref), channel_id=1, source_target_pairs={{1,2},{2,1},{3,4},{4,3},{5,6},{6,5},{7,8},{8,7},{9,10},{10,9},{11,... | collective-permute-start | bytes 589832 | tf_op jit(solution)/shard_map/ppermute | solution.py:251
  28.5 0.0 copy-start.12
  28.5 0.0 copy-done
  28.5 0.0 copy-done.2
  28.5 0.0 copy-done.6
  28.5 0.0 copy-done.7
  28.5 0.0 copy-done.4
  28.5 0.6 copy-done.12
  29.1 0.0 copy-start.8
  29.1 0.9 %copy-done.8 = bf16[256,256]{1,0:T(8,128)(2,1)S(1)} copy-done((bf16[256,256]{1,0:T(8,128)(2,1)S(1)}, bf16[256,256]{1,0:T(8,128)(2,1)}, u32[]{:S(2)}) %copy-start.8) | copy-done | bytes 131096
  30.0 0.0 copy-start.1
  30.0 5.7 %shard_map.120 = (bf16[1536,128]{1,0:T(8,128)(2,1)S(1)}, bf16[1536,256]{1,0:T(8,128)(2,1)S(1)}) custom-call(bf16[16,48,128]{2,1,0:T(8,128)(2,1)S(1)} %all-to-all-done.latent_ref, bf16[16,128]{1,0:T(8,128)(2,1)S(1)} %copy-done.4, bf16[128,3072]{1,0:T(8,128)(2,1)S(1)} %copy-done, bf16[64,3072]{1,0:T(8,128)(2,1)S(1)} %copy-done.2, ...), custom_call_target="tpu_custom_call" | custom-call | flops 48318382080 | bytes 4194304 | tf_op jit(solution)/shard_map/pallas_call | solution.py:288
  35.8 0.0 copy-start.9
  35.8 0.0 copy-start.10
  35.8 0.0 copy-start.11
  35.8 3.3 %collective-permute-start = (bf16[1536,256]{1,0:T(8,128)(2,1)S(1)}, bf16[1536,256]{1,0:T(8,128)(2,1)S(1)}, u32[]{:S(2)}, u32[]{:S(2)}) collective-permute-start(bf16[1536,256]{1,0:T(8,128)(2,1)S(1)} %get-tuple-element.19.own_ref), channel_id=1, source_target_pairs={{0,1},{1,0},{2,3},{3,2},{4,5},{5,4},{6,7},{7,6},{8,9},{9,8},{10,11... | collective-permute-start | bytes 2359304 | tf_op jit(solution)/shard_map/ppermute | solution.py:295
  39.0 0.0 collective-permute-done.1.latent_ref
  39.1 0.0 copy-done.1
  39.1 5.4 %shard_map.121.outer_ref = bf16[1536,256]{1,0:T(8,128)(2,1)S(1)} custom-call(bf16[16,48,128]{2,1,0:T(8,128)(2,1)S(1)} %collective-permute-done.1.latent_ref, bf16[16,128]{1,0:T(8,128)(2,1)S(1)} %copy-done.4, bf16[128,3072]{1,0:T(8,128)(2,1)S(1)} %copy-done, bf16[64,3072]{1,0:T(8,128)(2,1)S(1)} %copy-done.2, bf16[3072,128]{1,0:T(8,128)(2,1)S(1)} %bitcast.20, ...), custom_call_target="tpu_custom_call" | custom-call | flops 48318382080 | bytes 4194304 | tf_op jit(solution)/shard_map/pallas_call | solution.py:296
  44.5 0.0 collective-permute-done.inner_ref
  44.5 0.0 copy-done.9
  44.5 0.0 copy-done.10
  44.5 0.0 copy-done.11
  44.5 2.3 %shard_map.122 = bf16[16,48,128]{2,1,0:T(8,128)(2,1)S(1)} custom-call(bf16[1536,128]{1,0:T(8,128)(2,1)S(1)} %get-tuple-element.18.query_ref, bf16[1536,256]{1,0:T(8,128)(2,1)S(1)} %get-tuple-element.19.own_ref, bf16[1536,256]{1,0:T(8,128)(2,1)S(1)} %collective-permute-done.inner_ref, bf16[1536,256]{1,0:T(8,128)(2,1)S(1)} %shard_map.121.outer_ref, ...), custom_call_target="tpu_custom_call" | custom-call | flops 6039797760 | bytes 4194304 | tf_op jit(solution)/shard_map/pallas_call | solution.py:303
  46.8 14.6 %all_to_all.10.taken_ref = bf16[16,48,128]{2,1,0:T(8,128)(2,1)S(1)} all-to-all(bf16[16,48,128]{2,1,0:T(8,128)(2,1)S(1)} %shard_map.122), channel_id=1, replica_groups=mesh['tm'=16,'ctx'=32] {'tm'}, dimensions={0} | all-to-all | bytes 393216 | tf_op jit(solution)/shard_map/all_to_all | solution.py:311
  61.3 0.8 %shard_map.123 = f32[64,96]{1,0:T(8,128)} custom-call(bf16[16,48,128]{2,1,0:T(8,128)(2,1)S(1)} %all_to_all.10.taken_ref, bf16[16,48,128]{2,1,0:T(8,128)(2,1)S(1)} %all-to-all-done.latent_ref), custom_call_target="tpu_custom_call" | custom-call | tf_op jit(solution)/shard_map/pallas_call | solution.py:312
  (2 shorter events, 0.0 us)
Async XLA Ops:
  0.0 0.8 %copy-start.3 = (f32[1,96,64]{1,2,0:T(8,128)S(1)}, f32[1,96,64]{1,2,0:T(8,128)}, u32[]{:S(2)}) copy-start(f32[1,96,64]{1,2,0:T(8,128)} %param.12) | copy-start | bytes 73732
  1.6 0.6 copy-start.5
  2.2 18.1 %all-to-all-start = ((bf16[16,48,128]{2,1,0:T(8,128)(2,1)}), bf16[16,48,128]{2,1,0:T(8,128)(2,1)S(1)}, u32[]{:S(2)}, u32[]{:S(2)}) async-start(bf16[16,48,128]{2,1,0:T(8,128)(2,1)} %get-tuple-element.14), calls=%async_computation | async-start | bytes 393216 | tf_op jit(solution)/shard_map/all_to_all | solution.py:249
  10.7 0.7 %copy-start.13 = (s32[17]{0:T(128)S(1)}, s32[17]{0:T(128)}, u32[]{:S(2)}) copy-start(s32[17]{0:T(128)} %plan_ref.1) | copy-start | bytes 208
  12.1 16.4 %copy-start = (bf16[128,3072]{1,0:T(8,128)(2,1)S(1)}, bf16[128,3072]{1,0:T(8,128)(2,1)}, u32[]{:S(2)}) copy-start(bf16[128,3072]{1,0:T(8,128)(2,1)} %time_ref.3) | copy-start | bytes 2359300
  12.1 16.4 %copy-start.2 = (bf16[64,3072]{1,0:T(8,128)(2,1)S(1)}, bf16[64,3072]{1,0:T(8,128)(2,1)}, u32[]{:S(2)}) copy-start(bf16[64,3072]{1,0:T(8,128)(2,1)} %embed_ref.3) | copy-start | bytes 1179652
  12.1 16.4 %copy-start.6 = (bf16[1,3072,128]{2,1,0:T(8,128)(2,1)S(1)}, bf16[1,3072,128]{2,1,0:T(8,128)(2,1)}, u32[]{:S(2)}) copy-start(bf16[1,3072,128]{2,1,0:T(8,128)(2,1)} %param.17) | copy-start | bytes 2359300
  12.1 16.4 %copy-start.7 = (bf16[1,3072,128]{2,1,0:T(8,128)(2,1)S(1)}, bf16[1,3072,128]{2,1,0:T(8,128)(2,1)}, u32[]{:S(2)}) copy-start(bf16[1,3072,128]{2,1,0:T(8,128)(2,1)} %param.18) | copy-start | bytes 2359300
  17.3 11.2 %copy-start.4 = (bf16[16,128]{1,0:T(8,128)(2,1)S(1)}, bf16[16,128]{1,0:T(8,128)(2,1)}, u32[]{:S(2)}) copy-start(bf16[16,128]{1,0:T(8,128)(2,1)} %pad_maximum_fusion.feature_ref) | copy-start | bytes 12292
  20.3 18.8 %collective-permute-start.1 = (bf16[16,48,128]{2,1,0:T(8,128)(2,1)S(1)}, bf16[16,48,128]{2,1,0:T(8,128)(2,1)S(1)}, u32[]{:S(2)}, u32[]{:S(2)}) collective-permute-start(bf16[16,48,128]{2,1,0:T(8,128)(2,1)S(1)} %all-to-all-done.latent_ref), channel_id=1, source_target_pairs={{1,2},{2,1},{3,4},{4,3},{5,6},{6,5},{7,8},{8,7},{9,10},{10,9},{11,... | collective-permute-start | bytes 589832 | tf_op jit(solution)/shard_map/ppermute | solution.py:251
  28.5 0.7 %copy-start.12 = (f32[2,128]{1,0:T(2,128)S(1)}, f32[2,128]{1,0:T(2,128)}, u32[]{:S(2)}) copy-start(f32[2,128]{1,0:T(2,128)} %get-tuple-element.16.gains) | copy-start | bytes 3076
  29.1 0.9 %copy-start.8 = (bf16[256,256]{1,0:T(8,128)(2,1)S(1)}, bf16[256,256]{1,0:T(8,128)(2,1)}, u32[]{:S(2)}) copy-start(bf16[256,256]{1,0:T(8,128)(2,1)} %get-tuple-element.17.rest_0_) | copy-start | bytes 393220
  30.0 9.0 %copy-start.1 = (bf16[1,3072,128]{2,1,0:T(8,128)(2,1)S(1)}, bf16[1,3072,128]{2,1,0:T(8,128)(2,1)}, u32[]{:S(2)}) copy-start(bf16[1,3072,128]{2,1,0:T(8,128)(2,1)} %param.19) | copy-start | bytes 2359300
  35.8 8.7 %copy-start.9 = (bf16[256,128]{1,0:T(8,128)(2,1)S(1)}, bf16[256,128]{1,0:T(8,128)(2,1)}, u32[]{:S(2)}) copy-start(bf16[256,128]{1,0:T(8,128)(2,1)} %get-tuple-element.20.tail_ref) | copy-start | bytes 196612
  35.8 8.7 %copy-start.10 = (f32[48,128]{1,0:T(8,128)S(1)}, f32[48,128]{1,0:T(8,128)}, u32[]{:S(2)}) copy-start(f32[48,128]{1,0:T(8,128)} %get-tuple-element.21.extra_ref) | copy-start | bytes 73732
  35.8 8.7 %copy-start.11 = (f32[16,128]{1,0:T(8,128)S(1)}, f32[16,128]{1,0:T(8,128)}, u32[]{:S(2)}) copy-start(f32[16,128]{1,0:T(8,128)} %get-tuple-element.22.sizes) | copy-start | bytes 24580
  35.8 8.7 %collective-permute-start = (bf16[1536,256]{1,0:T(8,128)(2,1)S(1)}, bf16[1536,256]{1,0:T(8,128)(2,1)S(1)}, u32[]{:S(2)}, u32[]{:S(2)}) collective-permute-start(bf16[1536,256]{1,0:T(8,128)(2,1)S(1)} %get-tuple-element.19.own_ref), channel_id=1, source_target_pairs={{0,1},{1,0},{2,3},{3,2},{4,5},{5,4},{6,7},{7,6},{8,9},{9,8},{10,11... | collective-permute-start | bytes 2359304 | tf_op jit(solution)/shard_map/ppermute | solution.py:295

commit v3 on v2

--- a/solution.py
+++ b/solution.py
@@ -10,7 +10,7 @@
 
 F32, BF16 = jnp.float32, jnp.bfloat16
 MIB = 1 << 20
-FOLD_LIMIT = 54
+FOLD_LIMIT = 53
 VMEM = pl.BlockSpec(memory_space=pltpu.VMEM)
 HBM = pl.BlockSpec(memory_space=pltpu.HBM)
 SMEM = pl.BlockSpec(memory_space=pltpu.SMEM)
@@ -33,11 +33,10 @@
     return high, (value - high.astype(F32)).astype(BF16)
 
 
-def pack_kernel(state_ref, own_ref, copies_ref):
+def pack_kernel(state_ref, copies_ref):
     rows = state_ref[...].T.astype(BF16)
     half = rows.shape[0] // 2
     packed = jnp.concatenate([rows[:half], rows[half:]], axis=1)
-    own_ref[...] = packed
     copies_ref[...] = jnp.broadcast_to(packed[None], copies_ref.shape)
 
 
@@ -51,7 +50,6 @@
 
 def fold_kernel(
     plan_ref,
-    own_ref,
     feature_ref,
     state_ref,
     noise_ref,
@@ -91,7 +89,10 @@
     features = feature_ref[...].astype(F32)
     chosen = lax.broadcasted_iota(jnp.int32, features.shape, 0) == mine
     features = jnp.sum(jnp.where(chosen, features, 0.0), axis=0, keepdims=True).astype(BF16)
-    taken = input_rows(own_ref[...], features)
+    state = state_ref[...].T
+    rows = state.astype(BF16)
+    features = jnp.broadcast_to(features, (rows.shape[0], freq))
+    taken = jnp.concatenate([features, rows], axis=1)
     for s in range(sizes.shape[0]):
         size = (plan_ref[s] - plan_ref[s + 1]).astype(F32) / 1000.0
         sizes[s : s + 1, :] = jnp.full((1, sizes.shape[1]), size, F32)
@@ -105,10 +106,9 @@
     into_value[:, width:] = jnp.concatenate([low, low[freq:]], axis=0)
     product = lax.dot_general(left, final, NT, preferred_element_type=F32)
     product = jnp.concatenate(split(product), axis=1)
-    residual = dot(taken, jnp.concatenate([product, product[freq:]], axis=0))
+    residual = dot(taken, product)
     residual = residual[:, :channels] + residual[:, channels:]
-    state = state_ref[...].T
-    rest = state - state.astype(BF16).astype(F32)
+    rest = state - rows.astype(F32)
     extra = size * residual + jnp.sqrt(size) * noise_ref[...].T + jnp.where(mine == 0, rest, 0.0)
     half = extra.shape[0] // 2
     extra_ref[...] = jnp.concatenate([extra[:half], extra[half:]], axis=1)
@@ -243,9 +243,7 @@
     packed = (steps, tile // 2, 2 * channels)
     features = fourier_rows(plan, freq, steps)
 
-    own, copies = call(
-        pack_kernel, [struct(packed[1:], BF16), struct(packed, BF16)], [VMEM], limit=8
-    )(state)
+    copies = call(pack_kernel, struct(packed, BF16), [VMEM], limit=8)(state)
     latents = lax.all_to_all(copies, "tm", 0, 0, tiled=True)
     outward = [(i, i + 1 if i % 2 else i - 1) for i in range(1, count - 1)]
     outer_latents = lax.ppermute(latents, "ctx", outward)
@@ -259,7 +257,7 @@
             struct((2, width), F32),
             struct((steps, 2 * channels), F32),
         ],
-        [SMEM] + [VMEM] * 4 + [HBM] * 7,
+        [SMEM] + [VMEM] * 3 + [HBM] * 7,
         [
             pltpu.VMEM((freq + channels, depth), BF16),
             pltpu.VMEM((depth, width), BF16),
@@ -272,7 +270,6 @@
         moved=1024,
     )(
         plan,
-        own,
         features,
         state,
         noise,
@@ -286,7 +283,7 @@
     )
     flops = 40 * rows * depth * 256
     query, own_pair = call(
-        functools.partial(project_kernel, True, 4, 256),
+        functools.partial(project_kernel, True, 8, 256),
         [struct((rows, width), BF16), struct((rows, 2 * width), BF16)],
         [VMEM] * 8,
         flops=flops,
@@ -301,7 +298,7 @@
         moved=4 * MIB,
     )(outer_latents, features, w_time, w_embed, w_key[0], w_value[0], gains)
     sent = call(
-        functools.partial(attend_kernel, 4),
+        functools.partial(attend_kernel, 8),
         struct(packed, BF16),
         [VMEM] * 7,
         [pltpu.VMEM((rows, 3 * tile), F32)],

time: 62.5 us -> 60.8 us (0.973)
  the two profiles are of different devices: /device:TPU:24 before, /device:TPU:1 now
where the time goes in v3:
time: 60.8 us; the launch traced here: 60.4 us
  starting transfers between devices  22.2 us (37%)
  Pallas kernels  18.6 us (31%)
  blocking collectives  12.7 us (21%)
  waiting for transfers between devices  4.91 us (8%)
  local copies, waits for them, and re-layouts  1.51 us (2%)
    all_to_all x1, blocking collectives, per_device(): taken = lax.all_to_all(sent, 'tm', 0, 0, tiled=True)  12.7 us
    ppermute x1, starting transfers between devices, per_device(): outer_latents = lax.ppermute(latents, 'ctx', outward)  11 us
    all_to_all x1, starting transfers between devices, per_device(): latents = lax.all_to_all(copies, 'tm', 0, 0, tiled=True)  9.15 us
    pallas_call x1, Pallas kernels, per_device(): call(functools.partial(project_kernel, True, 8, 256), [struct((rows, widt...  5.49 us
    pallas_call x1, Pallas kernels, per_device(): call(functools.partial(project_kernel, False, 4, 256), struct((rows, 2 *...  5.41 us
    pallas_call x1, Pallas kernels, per_device(): call(fold_kernel, [struct((inputs, 2 * width), BF16), struct((2 * width,...  4.2 us
    all_to_all x1, waiting for transfers between devices, per_device(): latents = lax.all_to_all(copies, 'tm', 0, 0, tiled=True)  3.17 us
    ppermute x1, starting transfers between devices, per_device(): lax.ppermute(own_pair, 'ctx', [(i, i ^ 1) for i in range(count)])  2.1 us
  transfers between devices with their start and end apart: 3, of which 2 were waited for; matrix products, arithmetic and copies ran while one was open for 0% of the time, Pallas kernels for 25%

profile of v3, /device:TPU:1, one launch (start us, length us, event | category | flops | bytes accessed | tf_op | source)
XLA Modules:
  0.0 60.4 jit_solution(1103363264955129638)
XLA Ops:
  0.0 0.0 copy-start.2
  0.0 0.0 copy-start.3
  0.0 0.8 %copy-done.3 = f32[1,96,64]{1,2,0:T(8,128)S(1)} copy-done((f32[1,96,64]{1,2,0:T(8,128)S(1)}, f32[1,96,64]{1,2,0:T(8,128)}, u32[]{:S(2)}) %copy-start.3) | copy-done | bytes 24600
  0.8 0.8 %shard_map.118 = bf16[16,48,128]{2,1,0:T(8,128)(2,1)} custom-call(f32[64,96]{1,0:T(8,128)S(1)} %bitcast.16), custom_call_target="tpu_custom_call" | custom-call | tf_op jit(solution)/shard_map/pallas_call | solution.py:246
  1.7 0.0 copy-start.6
  1.7 0.0 copy-start.5
  1.7 9.1 %all-to-all-start = ((bf16[16,48,128]{2,1,0:T(8,128)(2,1)}), bf16[16,48,128]{2,1,0:T(8,128)(2,1)S(1)}, u32[]{:S(2)}, u32[]{:S(2)}) async-start(bf16[16,48,128]{2,1,0:T(8,128)(2,1)} %shard_map.118), calls=%async_computation | async-start | bytes 393216 | tf_op jit(solution)/shard_map/all_to_all | solution.py:247
  10.8 0.0 copy-start.4
  10.8 0.0 copy-done.6
  10.9 0.1 fusion
  11.0 0.1 pad_maximum_fusion.feature_ref
  11.1 0.0 copy-start.7
  11.1 0.0 copy-start.8
  11.1 0.0 copy-done.2
  11.1 0.0 copy-done.5
  11.1 0.5 copy-done.4
  11.6 0.1 copy-done.7
  11.7 0.0 copy-done.8
  11.7 0.0 copy-start
  11.7 0.0 copy-start.9
  11.7 0.0 copy-start.10
  11.8 4.2 %shard_map.119 = (bf16[256,256]{1,0:T(8,128)(2,1)S(1)}, bf16[256,128]{1,0:T(8,128)(2,1)S(1)}, f32[48,128]{1,0:T(8,128)S(1)}, f32[2,128]{1,0:T(2,128)S(1)}, f32[16,128]{1,0:T(8,128)S(1)}) custom-call(s32[17]{0:T(128)S(1)} %copy-done.6, bf16[16,128]{1,0:T(8,128)(2,1)S(1)} %pad_maximum_fusion.feature_ref, f32[64,96]{1,0:T(8,128)S(1)} %bitcast.17, ...), custom_call_target="tpu_custom_call" | custom-call | flops 1048576 | bytes 1024 | tf_op jit(solution)/shard_map/pallas_call | solution.py:251
  16.0 3.2 %all-to-all-done.latent_ref = bf16[16,48,128]{2,1,0:T(8,128)(2,1)S(1)} async-done(((bf16[16,48,128]{2,1,0:T(8,128)(2,1)}), bf16[16,48,128]{2,1,0:T(8,128)(2,1)S(1)}, u32[]{:S(2)}, u32[]{:S(2)}) %all-to-all-start) | async-done | bytes 196640 | tf_op jit(solution)/shard_map/all_to_all | solution.py:247
  19.1 11.0 %collective-permute-start.1 = (bf16[16,48,128]{2,1,0:T(8,128)(2,1)S(1)}, bf16[16,48,128]{2,1,0:T(8,128)(2,1)S(1)}, u32[]{:S(2)}, u32[]{:S(2)}) collective-permute-start(bf16[16,48,128]{2,1,0:T(8,128)(2,1)S(1)} %all-to-all-done.latent_ref), channel_id=1, source_target_pairs={{1,2},{2,1},{3,4},{4,3},{5,6},{6,5},{7,8},{8,7},{9,10},{10,9},{11,... | collective-permute-start | bytes 589832 | tf_op jit(solution)/shard_map/ppermute | solution.py:249
  30.1 0.0 copy-done
  30.1 0.0 copy-done.9
  30.1 0.0 copy-done.10
  30.1 0.0 copy-start.1
  30.1 5.5 %shard_map.120 = (bf16[1536,128]{1,0:T(8,128)(2,1)S(1)}, bf16[1536,256]{1,0:T(8,128)(2,1)S(1)}) custom-call(bf16[16,48,128]{2,1,0:T(8,128)(2,1)S(1)} %all-to-all-done.latent_ref, bf16[16,128]{1,0:T(8,128)(2,1)S(1)} %pad_maximum_fusion.feature_ref, bf16[128,3072]{1,0:T(8,128)(2,1)S(1)} %copy-done, bf16[64,3072]{1,0:T(8,128)(2,1)S(1)} %copy-done.2, ...), custom_call_target="tpu_custom_call" | custom-call | flops 48318382080 | bytes 4194304 | tf_op jit(solution)/shard_map/pallas_call | solution.py:285
  35.6 2.1 %collective-permute-start = (bf16[1536,256]{1,0:T(8,128)(2,1)S(1)}, bf16[1536,256]{1,0:T(8,128)(2,1)S(1)}, u32[]{:S(2)}, u32[]{:S(2)}) collective-permute-start(bf16[1536,256]{1,0:T(8,128)(2,1)S(1)} %get-tuple-element.15.own_ref), channel_id=1, source_target_pairs={{0,1},{1,0},{2,3},{3,2},{4,5},{5,4},{6,7},{7,6},{8,9},{9,8},{10,11... | collective-permute-start | bytes 2359304 | tf_op jit(solution)/shard_map/ppermute | solution.py:292
  37.7 1.7 %collective-permute-done.1.latent_ref = bf16[16,48,128]{2,1,0:T(8,128)(2,1)S(1)} collective-permute-done((bf16[16,48,128]{2,1,0:T(8,128)(2,1)S(1)}, bf16[16,48,128]{2,1,0:T(8,128)(2,1)S(1)}, u32[]{:S(2)}, u32[]{:S(2)}) %collective-permute-start.1) | collective-permute-done | bytes 196640 | tf_op jit(solution)/shard_map/ppermute | solution.py:249
  39.5 0.0 copy-done.1
  39.5 5.4 %shard_map.121.outer_ref = bf16[1536,256]{1,0:T(8,128)(2,1)S(1)} custom-call(bf16[16,48,128]{2,1,0:T(8,128)(2,1)S(1)} %collective-permute-done.1.latent_ref, bf16[16,128]{1,0:T(8,128)(2,1)S(1)} %pad_maximum_fusion.feature_ref, bf16[128,3072]{1,0:T(8,128)(2,1)S(1)} %copy-done, bf16[64,3072]{1,0:T(8,128)(2,1)S(1)} %copy-done.2, ...), custom_call_target="tpu_custom_call" | custom-call | flops 48318382080 | bytes 4194304 | tf_op jit(solution)/shard_map/pallas_call | solution.py:293
  44.9 0.0 collective-permute-done.inner_ref
  44.9 1.9 %shard_map.122 = bf16[16,48,128]{2,1,0:T(8,128)(2,1)S(1)} custom-call(bf16[1536,128]{1,0:T(8,128)(2,1)S(1)} %get-tuple-element.14.query_ref, bf16[1536,256]{1,0:T(8,128)(2,1)S(1)} %get-tuple-element.15.own_ref, bf16[1536,256]{1,0:T(8,128)(2,1)S(1)} %collective-permute-done.inner_ref, bf16[1536,256]{1,0:T(8,128)(2,1)S(1)} %shard_map.121.outer_ref, ...), custom_call_target="tpu_custom_call" | custom-call | flops 6039797760 | bytes 4194304 | tf_op jit(solution)/shard_map/pallas_call | solution.py:300
  46.8 12.7 %all_to_all.10.taken_ref = bf16[16,48,128]{2,1,0:T(8,128)(2,1)S(1)} all-to-all(bf16[16,48,128]{2,1,0:T(8,128)(2,1)S(1)} %shard_map.122), channel_id=1, replica_groups=mesh['tm'=16,'ctx'=32] {'tm'}, dimensions={0} | all-to-all | bytes 393216 | tf_op jit(solution)/shard_map/all_to_all | solution.py:308
  59.6 0.8 %shard_map.123 = f32[64,96]{1,0:T(8,128)} custom-call(bf16[16,48,128]{2,1,0:T(8,128)(2,1)S(1)} %all_to_all.10.taken_ref, bf16[16,48,128]{2,1,0:T(8,128)(2,1)S(1)} %all-to-all-done.latent_ref), custom_call_target="tpu_custom_call" | custom-call | tf_op jit(solution)/shard_map/pallas_call | solution.py:309
  (2 shorter events, 0.0 us)
Async XLA Ops:
  0.0 11.1 %copy-start.2 = (bf16[64,3072]{1,0:T(8,128)(2,1)S(1)}, bf16[64,3072]{1,0:T(8,128)(2,1)}, u32[]{:S(2)}) copy-start(bf16[64,3072]{1,0:T(8,128)(2,1)} %embed_ref.3) | copy-start | bytes 1179652
  0.0 0.8 %copy-start.3 = (f32[1,96,64]{1,2,0:T(8,128)S(1)}, f32[1,96,64]{1,2,0:T(8,128)}, u32[]{:S(2)}) copy-start(f32[1,96,64]{1,2,0:T(8,128)} %param.12) | copy-start | bytes 73732
  1.7 9.2 %copy-start.6 = (s32[17]{0:T(128)S(1)}, s32[17]{0:T(128)}, u32[]{:S(2)}) copy-start(s32[17]{0:T(128)} %plan_ref.1) | copy-start | bytes 208
  1.7 9.4 %copy-start.5 = (f32[1,96,64]{1,2,0:T(8,128)S(1)}, f32[1,96,64]{1,2,0:T(8,128)}, u32[]{:S(2)}) copy-start(f32[1,96,64]{1,2,0:T(8,128)} %param.13) | copy-start | bytes 73732
  1.7 17.5 %all-to-all-start = ((bf16[16,48,128]{2,1,0:T(8,128)(2,1)}), bf16[16,48,128]{2,1,0:T(8,128)(2,1)S(1)}, u32[]{:S(2)}, u32[]{:S(2)}) async-start(bf16[16,48,128]{2,1,0:T(8,128)(2,1)} %shard_map.118), calls=%async_computation | async-start | bytes 393216 | tf_op jit(solution)/shard_map/all_to_all | solution.py:247
  10.8 0.8 %copy-start.4 = (f32[1,96,64]{1,2,0:T(8,128)S(1)}, f32[1,96,64]{1,2,0:T(8,128)}, u32[]{:S(2)}) copy-start(f32[1,96,64]{1,2,0:T(8,128)} %param.12) | copy-start | bytes 73732
  11.1 0.7 %copy-start.7 = (f32[1,128]{1,0:T(1,128)S(1)}, f32[1,128]{1,0:T(1,128)}, u32[]{:S(2)}) copy-start(f32[1,128]{1,0:T(1,128)} %gain_query_hbm.1) | copy-start | bytes 1540
  11.1 0.7 %copy-start.8 = (f32[1,128]{1,0:T(1,128)S(1)}, f32[1,128]{1,0:T(1,128)}, u32[]{:S(2)}) copy-start(f32[1,128]{1,0:T(1,128)} %gain_key_hbm.1) | copy-start | bytes 1540
  11.7 18.4 %copy-start = (bf16[128,3072]{1,0:T(8,128)(2,1)S(1)}, bf16[128,3072]{1,0:T(8,128)(2,1)}, u32[]{:S(2)}) copy-start(bf16[128,3072]{1,0:T(8,128)(2,1)} %time_ref.3) | copy-start | bytes 2359300
  11.7 18.4 %copy-start.9 = (bf16[1,3072,128]{2,1,0:T(8,128)(2,1)S(1)}, bf16[1,3072,128]{2,1,0:T(8,128)(2,1)}, u32[]{:S(2)}) copy-start(bf16[1,3072,128]{2,1,0:T(8,128)(2,1)} %param.17) | copy-start | bytes 2359300
  11.7 18.4 %copy-start.10 = (bf16[1,3072,128]{2,1,0:T(8,128)(2,1)S(1)}, bf16[1,3072,128]{2,1,0:T(8,128)(2,1)}, u32[]{:S(2)}) copy-start(bf16[1,3072,128]{2,1,0:T(8,128)(2,1)} %param.18) | copy-start | bytes 2359300
  19.1 20.4 %collective-permute-start.1 = (bf16[16,48,128]{2,1,0:T(8,128)(2,1)S(1)}, bf16[16,48,128]{2,1,0:T(8,128)(2,1)S(1)}, u32[]{:S(2)}, u32[]{:S(2)}) collective-permute-start(bf16[16,48,128]{2,1,0:T(8,128)(2,1)S(1)} %all-to-all-done.latent_ref), channel_id=1, source_target_pairs={{1,2},{2,1},{3,4},{4,3},{5,6},{6,5},{7,8},{8,7},{9,10},{10,9},{11,... | collective-permute-start | bytes 589832 | tf_op jit(solution)/shard_map/ppermute | solution.py:249
  30.1 9.4 %copy-start.1 = (bf16[1,3072,128]{2,1,0:T(8,128)(2,1)S(1)}, bf16[1,3072,128]{2,1,0:T(8,128)(2,1)}, u32[]{:S(2)}) copy-start(bf16[1,3072,128]{2,1,0:T(8,128)(2,1)} %param.19) | copy-start | bytes 2359300
  35.6 9.3 %collective-permute-start = (bf16[1536,256]{1,0:T(8,128)(2,1)S(1)}, bf16[1536,256]{1,0:T(8,128)(2,1)S(1)}, u32[]{:S(2)}, u32[]{:S(2)}) collective-permute-start(bf16[1536,256]{1,0:T(8,128)(2,1)S(1)} %get-tuple-element.15.own_ref), channel_id=1, source_target_pairs={{0,1},{1,0},{2,3},{3,2},{4,5},{5,4},{6,7},{7,6},{8,9},{9,8},{10,11... | collective-permute-start | bytes 2359304 | tf_op jit(solution)/shard_map/ppermute | solution.py:292

commit v4 on v3

--- a/solution.py
+++ b/solution.py
@@ -67,7 +67,6 @@
     sizes,
     first,
     value_ref,
-    out_ref,
     final_ref,
     sems,
 ):
@@ -75,10 +74,10 @@
     channels = embed_hbm.shape[0]
     pairs = (
         (time_hbm, first.at[:freq]),
-        (embed_hbm, first.at[freq:]),
+        (embed_hbm, first.at[freq : freq + channels]),
         (value_hbm, value_ref),
         (final_hbm, final_ref),
-        (out_hbm, out_ref),
+        (out_hbm, first.at[freq + channels :]),
         (gain_query_hbm, gains.at[0:1]),
         (gain_key_hbm, gains.at[1:2]),
     )
@@ -98,23 +97,24 @@
         sizes[s : s + 1, :] = jnp.full((1, sizes.shape[1]), size, F32)
     size = (plan_ref[mine] - plan_ref[mine + 1]).astype(F32) / 1000.0
     size = jnp.full((taken.shape[0], channels), size, F32)
-    for copy in copies:
+    both = freq + channels
+    for copy in copies[:3]:
         copy.wait()
-    left, final = first[...], final_ref[...]
-    high, low = split(dot(left, value_ref[...]))
+    high, low = split(dot(first[:both, :], value_ref[...]))
     into_value[:, :width] = jnp.concatenate([high, high[freq:]], axis=0)
     into_value[:, width:] = jnp.concatenate([low, low[freq:]], axis=0)
-    product = lax.dot_general(left, final, NT, preferred_element_type=F32)
-    product = jnp.concatenate(split(product), axis=1)
-    residual = dot(taken, product)
+    for copy in copies[3:]:
+        copy.wait()
+    product = lax.dot_general(first[...], final_ref[...], NT, preferred_element_type=F32)
+    high, low = split(product)
+    tail[:width, :] = jnp.concatenate([high[both:], high[both:]], axis=1)
+    tail[width:, :] = jnp.concatenate([low[both:], low[both:]], axis=1)
+    residual = dot(taken, jnp.concatenate([high[:both], low[:both]], axis=1))
     residual = residual[:, :channels] + residual[:, channels:]
     rest = state - rows.astype(F32)
     extra = size * residual + jnp.sqrt(size) * noise_ref[...].T + jnp.where(mine == 0, rest, 0.0)
     half = extra.shape[0] // 2
     extra_ref[...] = jnp.concatenate([extra[:half], extra[half:]], axis=1)
-    high, low = split(lax.dot_general(out_ref[...], final, NT, preferred_element_type=F32))
-    tail[:width, :] = jnp.concatenate([high, high], axis=1)
-    tail[width:, :] = jnp.concatenate([low, low], axis=1)
 
 
 def rms_gain(values, gain):
@@ -259,9 +259,8 @@
         ],
         [SMEM] + [VMEM] * 3 + [HBM] * 7,
         [
-            pltpu.VMEM((freq + channels, depth), BF16),
+            pltpu.VMEM((freq + channels + width, depth), BF16),
             pltpu.VMEM((depth, width), BF16),
-            pltpu.VMEM((width, depth), BF16),
             pltpu.VMEM((channels, depth), BF16),
             pltpu.SemaphoreType.DMA((7,)),
         ],

time: 60.8 us -> 60.8 us (level)
  transfers between devices with their start and end apart: 3 -> 3, of which waited for: 2 -> 2; matrix products, arithmetic and copies ran while one was open for 0% -> 0% of each run, Pallas kernels for 25% -> 24%
where the time goes in v4:
time: 60.8 us; the launch traced here: 60.4 us
  starting transfers between devices  22.2 us (37%)
  Pallas kernels  18.1 us (30%)
  blocking collectives  12.7 us (21%)
  waiting for transfers between devices  5.42 us (9%)
  local copies, waits for them, and re-layouts  1.51 us (2%)
    all_to_all x1, blocking collectives, per_device(): taken = lax.all_to_all(sent, 'tm', 0, 0, tiled=True)  12.7 us
    ppermute x1, starting transfers between devices, per_device(): outer_latents = lax.ppermute(latents, 'ctx', outward)  11 us
    all_to_all x1, starting transfers between devices, per_device(): latents = lax.all_to_all(copies, 'tm', 0, 0, tiled=True)  9.15 us
    pallas_call x1, Pallas kernels, per_device(): call(functools.partial(project_kernel, True, 8, 256), [struct((rows, widt...  5.49 us
    pallas_call x1, Pallas kernels, per_device(): call(functools.partial(project_kernel, False, 4, 256), struct((rows, 2 *...  5.41 us
    all_to_all x1, waiting for transfers between devices, per_device(): latents = lax.all_to_all(copies, 'tm', 0, 0, tiled=True)  3.68 us
    pallas_call x1, Pallas kernels, per_device(): call(fold_kernel, [struct((inputs, 2 * width), BF16), struct((2 * width,...  3.68 us
    ppermute x1, starting transfers between devices, per_device(): lax.ppermute(own_pair, 'ctx', [(i, i ^ 1) for i in range(count)])  2.1 us
  transfers between devices with their start and end apart: 3, of which 2 were waited for; matrix products, arithmetic and copies ran while one was open for 0% of the time, Pallas kernels for 24%

profile of v4, /device:TPU:1, one launch (start us, length us, event | category | flops | bytes accessed | tf_op | source)
XLA Modules:
  0.0 60.4 jit_solution(13563814056509785912)
XLA Ops:
  0.0 0.0 copy-start.2
  0.0 0.0 copy-start.3
  0.0 0.8 %copy-done.3 = f32[1,96,64]{1,2,0:T(8,128)S(1)} copy-done((f32[1,96,64]{1,2,0:T(8,128)S(1)}, f32[1,96,64]{1,2,0:T(8,128)}, u32[]{:S(2)}) %copy-start.3) | copy-done | bytes 24600
  0.8 0.8 %shard_map.118 = bf16[16,48,128]{2,1,0:T(8,128)(2,1)} custom-call(f32[64,96]{1,0:T(8,128)S(1)} %bitcast.16), custom_call_target="tpu_custom_call" | custom-call | tf_op jit(solution)/shard_map/pallas_call | solution.py:246
  1.7 0.0 copy-start.6
  1.7 0.0 copy-start.5
  1.7 9.1 %all-to-all-start = ((bf16[16,48,128]{2,1,0:T(8,128)(2,1)}), bf16[16,48,128]{2,1,0:T(8,128)(2,1)S(1)}, u32[]{:S(2)}, u32[]{:S(2)}) async-start(bf16[16,48,128]{2,1,0:T(8,128)(2,1)} %shard_map.118), calls=%async_computation | async-start | bytes 393216 | tf_op jit(solution)/shard_map/all_to_all | solution.py:247
  10.8 0.0 copy-start.4
  10.8 0.0 copy-done.6
  10.9 0.1 fusion
  11.0 0.1 pad_maximum_fusion.feature_ref
  11.1 0.0 copy-start.7
  11.1 0.0 copy-start.8
  11.1 0.0 copy-done.2
  11.1 0.0 copy-done.5
  11.1 0.5 copy-done.4
  11.6 0.1 copy-done.7
  11.7 0.0 copy-done.8
  11.7 0.0 copy-start
  11.7 0.0 copy-start.9
  11.7 0.0 copy-start.10
  11.8 3.7 %shard_map.119 = (bf16[256,256]{1,0:T(8,128)(2,1)S(1)}, bf16[256,128]{1,0:T(8,128)(2,1)S(1)}, f32[48,128]{1,0:T(8,128)S(1)}, f32[2,128]{1,0:T(2,128)S(1)}, f32[16,128]{1,0:T(8,128)S(1)}) custom-call(s32[17]{0:T(128)S(1)} %copy-done.6, bf16[16,128]{1,0:T(8,128)(2,1)S(1)} %pad_maximum_fusion.feature_ref, f32[64,96]{1,0:T(8,128)S(1)} %bitcast.17, ...), custom_call_target="tpu_custom_call" | custom-call | flops 1048576 | bytes 1024 | tf_op jit(solution)/shard_map/pallas_call | solution.py:251
  15.4 3.7 %all-to-all-done.latent_ref = bf16[16,48,128]{2,1,0:T(8,128)(2,1)S(1)} async-done(((bf16[16,48,128]{2,1,0:T(8,128)(2,1)}), bf16[16,48,128]{2,1,0:T(8,128)(2,1)S(1)}, u32[]{:S(2)}, u32[]{:S(2)}) %all-to-all-start) | async-done | bytes 196640 | tf_op jit(solution)/shard_map/all_to_all | solution.py:247
  19.1 11.0 %collective-permute-start.1 = (bf16[16,48,128]{2,1,0:T(8,128)(2,1)S(1)}, bf16[16,48,128]{2,1,0:T(8,128)(2,1)S(1)}, u32[]{:S(2)}, u32[]{:S(2)}) collective-permute-start(bf16[16,48,128]{2,1,0:T(8,128)(2,1)S(1)} %all-to-all-done.latent_ref), channel_id=1, source_target_pairs={{1,2},{2,1},{3,4},{4,3},{5,6},{6,5},{7,8},{8,7},{9,10},{10,9},{11,... | collective-permute-start | bytes 589832 | tf_op jit(solution)/shard_map/ppermute | solution.py:249
  30.1 0.0 copy-done
  30.1 0.0 copy-done.9
  30.1 0.0 copy-done.10
  30.1 0.0 copy-start.1
  30.1 5.5 %shard_map.120 = (bf16[1536,128]{1,0:T(8,128)(2,1)S(1)}, bf16[1536,256]{1,0:T(8,128)(2,1)S(1)}) custom-call(bf16[16,48,128]{2,1,0:T(8,128)(2,1)S(1)} %all-to-all-done.latent_ref, bf16[16,128]{1,0:T(8,128)(2,1)S(1)} %pad_maximum_fusion.feature_ref, bf16[128,3072]{1,0:T(8,128)(2,1)S(1)} %copy-done, bf16[64,3072]{1,0:T(8,128)(2,1)S(1)} %copy-done.2, ...), custom_call_target="tpu_custom_call" | custom-call | flops 48318382080 | bytes 4194304 | tf_op jit(solution)/shard_map/pallas_call | solution.py:284
  35.6 2.1 %collective-permute-start = (bf16[1536,256]{1,0:T(8,128)(2,1)S(1)}, bf16[1536,256]{1,0:T(8,128)(2,1)S(1)}, u32[]{:S(2)}, u32[]{:S(2)}) collective-permute-start(bf16[1536,256]{1,0:T(8,128)(2,1)S(1)} %get-tuple-element.15.own_ref), channel_id=1, source_target_pairs={{0,1},{1,0},{2,3},{3,2},{4,5},{5,4},{6,7},{7,6},{8,9},{9,8},{10,11... | collective-permute-start | bytes 2359304 | tf_op jit(solution)/shard_map/ppermute | solution.py:291
  37.7 1.7 %collective-permute-done.1.latent_ref = bf16[16,48,128]{2,1,0:T(8,128)(2,1)S(1)} collective-permute-done((bf16[16,48,128]{2,1,0:T(8,128)(2,1)S(1)}, bf16[16,48,128]{2,1,0:T(8,128)(2,1)S(1)}, u32[]{:S(2)}, u32[]{:S(2)}) %collective-permute-start.1) | collective-permute-done | bytes 196640 | tf_op jit(solution)/shard_map/ppermute | solution.py:249
  39.5 0.0 copy-done.1
  39.5 5.4 %shard_map.121.outer_ref = bf16[1536,256]{1,0:T(8,128)(2,1)S(1)} custom-call(bf16[16,48,128]{2,1,0:T(8,128)(2,1)S(1)} %collective-permute-done.1.latent_ref, bf16[16,128]{1,0:T(8,128)(2,1)S(1)} %pad_maximum_fusion.feature_ref, bf16[128,3072]{1,0:T(8,128)(2,1)S(1)} %copy-done, bf16[64,3072]{1,0:T(8,128)(2,1)S(1)} %copy-done.2, ...), custom_call_target="tpu_custom_call" | custom-call | flops 48318382080 | bytes 4194304 | tf_op jit(solution)/shard_map/pallas_call | solution.py:292
  44.9 0.0 collective-permute-done.inner_ref
  44.9 1.9 %shard_map.122 = bf16[16,48,128]{2,1,0:T(8,128)(2,1)S(1)} custom-call(bf16[1536,128]{1,0:T(8,128)(2,1)S(1)} %get-tuple-element.14.query_ref, bf16[1536,256]{1,0:T(8,128)(2,1)S(1)} %get-tuple-element.15.own_ref, bf16[1536,256]{1,0:T(8,128)(2,1)S(1)} %collective-permute-done.inner_ref, bf16[1536,256]{1,0:T(8,128)(2,1)S(1)} %shard_map.121.outer_ref, ...), custom_call_target="tpu_custom_call" | custom-call | flops 6039797760 | bytes 4194304 | tf_op jit(solution)/shard_map/pallas_call | solution.py:299
  46.8 12.7 %all_to_all.10.taken_ref = bf16[16,48,128]{2,1,0:T(8,128)(2,1)S(1)} all-to-all(bf16[16,48,128]{2,1,0:T(8,128)(2,1)S(1)} %shard_map.122), channel_id=1, replica_groups=mesh['tm'=16,'ctx'=32] {'tm'}, dimensions={0} | all-to-all | bytes 393216 | tf_op jit(solution)/shard_map/all_to_all | solution.py:307
  59.6 0.8 %shard_map.123 = f32[64,96]{1,0:T(8,128)} custom-call(bf16[16,48,128]{2,1,0:T(8,128)(2,1)S(1)} %all_to_all.10.taken_ref, bf16[16,48,128]{2,1,0:T(8,128)(2,1)S(1)} %all-to-all-done.latent_ref), custom_call_target="tpu_custom_call" | custom-call | tf_op jit(solution)/shard_map/pallas_call | solution.py:308
  (2 shorter events, 0.0 us)
Async XLA Ops:
  0.0 11.1 %copy-start.2 = (bf16[64,3072]{1,0:T(8,128)(2,1)S(1)}, bf16[64,3072]{1,0:T(8,128)(2,1)}, u32[]{:S(2)}) copy-start(bf16[64,3072]{1,0:T(8,128)(2,1)} %embed_ref.3) | copy-start | bytes 1179652
  0.0 0.8 %copy-start.3 = (f32[1,96,64]{1,2,0:T(8,128)S(1)}, f32[1,96,64]{1,2,0:T(8,128)}, u32[]{:S(2)}) copy-start(f32[1,96,64]{1,2,0:T(8,128)} %param.12) | copy-start | bytes 73732
  1.7 9.2 %copy-start.6 = (s32[17]{0:T(128)S(1)}, s32[17]{0:T(128)}, u32[]{:S(2)}) copy-start(s32[17]{0:T(128)} %plan_ref.1) | copy-start | bytes 208
  1.7 9.4 %copy-start.5 = (f32[1,96,64]{1,2,0:T(8,128)S(1)}, f32[1,96,64]{1,2,0:T(8,128)}, u32[]{:S(2)}) copy-start(f32[1,96,64]{1,2,0:T(8,128)} %param.13) | copy-start | bytes 73732
  1.7 17.5 %all-to-all-start = ((bf16[16,48,128]{2,1,0:T(8,128)(2,1)}), bf16[16,48,128]{2,1,0:T(8,128)(2,1)S(1)}, u32[]{:S(2)}, u32[]{:S(2)}) async-start(bf16[16,48,128]{2,1,0:T(8,128)(2,1)} %shard_map.118), calls=%async_computation | async-start | bytes 393216 | tf_op jit(solution)/shard_map/all_to_all | solution.py:247
  10.8 0.8 %copy-start.4 = (f32[1,96,64]{1,2,0:T(8,128)S(1)}, f32[1,96,64]{1,2,0:T(8,128)}, u32[]{:S(2)}) copy-start(f32[1,96,64]{1,2,0:T(8,128)} %param.12) | copy-start | bytes 73732
  11.1 0.7 %copy-start.7 = (f32[1,128]{1,0:T(1,128)S(1)}, f32[1,128]{1,0:T(1,128)}, u32[]{:S(2)}) copy-start(f32[1,128]{1,0:T(1,128)} %gain_query_hbm.1) | copy-start | bytes 1540
  11.1 0.7 %copy-start.8 = (f32[1,128]{1,0:T(1,128)S(1)}, f32[1,128]{1,0:T(1,128)}, u32[]{:S(2)}) copy-start(f32[1,128]{1,0:T(1,128)} %gain_key_hbm.1) | copy-start | bytes 1540
  11.7 18.4 %copy-start = (bf16[128,3072]{1,0:T(8,128)(2,1)S(1)}, bf16[128,3072]{1,0:T(8,128)(2,1)}, u32[]{:S(2)}) copy-start(bf16[128,3072]{1,0:T(8,128)(2,1)} %time_ref.3) | copy-start | bytes 2359300
  11.7 18.4 %copy-start.9 = (bf16[1,3072,128]{2,1,0:T(8,128)(2,1)S(1)}, bf16[1,3072,128]{2,1,0:T(8,128)(2,1)}, u32[]{:S(2)}) copy-start(bf16[1,3072,128]{2,1,0:T(8,128)(2,1)} %param.17) | copy-start | bytes 2359300
  11.7 18.4 %copy-start.10 = (bf16[1,3072,128]{2,1,0:T(8,128)(2,1)S(1)}, bf16[1,3072,128]{2,1,0:T(8,128)(2,1)}, u32[]{:S(2)}) copy-start(bf16[1,3072,128]{2,1,0:T(8,128)(2,1)} %param.18) | copy-start | bytes 2359300
  19.1 20.4 %collective-permute-start.1 = (bf16[16,48,128]{2,1,0:T(8,128)(2,1)S(1)}, bf16[16,48,128]{2,1,0:T(8,128)(2,1)S(1)}, u32[]{:S(2)}, u32[]{:S(2)}) collective-permute-start(bf16[16,48,128]{2,1,0:T(8,128)(2,1)S(1)} %all-to-all-done.latent_ref), channel_id=1, source_target_pairs={{1,2},{2,1},{3,4},{4,3},{5,6},{6,5},{7,8},{8,7},{9,10},{10,9},{11,... | collective-permute-start | bytes 589832 | tf_op jit(solution)/shard_map/ppermute | solution.py:249
  30.1 9.4 %copy-start.1 = (bf16[1,3072,128]{2,1,0:T(8,128)(2,1)S(1)}, bf16[1,3072,128]{2,1,0:T(8,128)(2,1)}, u32[]{:S(2)}) copy-start(bf16[1,3072,128]{2,1,0:T(8,128)(2,1)} %param.19) | copy-start | bytes 2359300
  35.6 9.3 %collective-permute-start = (bf16[1536,256]{1,0:T(8,128)(2,1)S(1)}, bf16[1536,256]{1,0:T(8,128)(2,1)S(1)}, u32[]{:S(2)}, u32[]{:S(2)}) collective-permute-start(bf16[1536,256]{1,0:T(8,128)(2,1)S(1)} %get-tuple-element.15.own_ref), channel_id=1, source_target_pairs={{0,1},{1,0},{2,3},{3,2},{4,5},{5,4},{6,7},{7,6},{8,9},{9,8},{10,11... | collective-permute-start | bytes 2359304 | tf_op jit(solution)/shard_map/ppermute | solution.py:291

commit v5 on v4

--- a/solution.py
+++ b/solution.py
@@ -297,7 +297,7 @@
         moved=4 * MIB,
     )(outer_latents, features, w_time, w_embed, w_key[0], w_value[0], gains)
     sent = call(
-        functools.partial(attend_kernel, 8),
+        functools.partial(attend_kernel, 16),
         struct(packed, BF16),
         [VMEM] * 7,
         [pltpu.VMEM((rows, 3 * tile), F32)],

time: 60.8 us -> 60.6 us (level)
  no operation moved by 1% of the time
where the time goes in v5:
time: 60.6 us; the launch traced here: 60.2 us
  starting transfers between devices  22.2 us (37%)
  Pallas kernels  18 us (30%)
  blocking collectives  12.7 us (21%)
  waiting for transfers between devices  5.42 us (9%)
  local copies, waits for them, and re-layouts  1.51 us (2%)
    all_to_all x1, blocking collectives, per_device(): taken = lax.all_to_all(sent, 'tm', 0, 0, tiled=True)  12.7 us
    ppermute x1, starting transfers between devices, per_device(): outer_latents = lax.ppermute(latents, 'ctx', outward)  11 us
    all_to_all x1, starting transfers between devices, per_device(): latents = lax.all_to_all(copies, 'tm', 0, 0, tiled=True)  9.15 us
    pallas_call x1, Pallas kernels, per_device(): call(functools.partial(project_kernel, True, 8, 256), [struct((rows, widt...  5.49 us
    pallas_call x1, Pallas kernels, per_device(): call(functools.partial(project_kernel, False, 4, 256), struct((rows, 2 *...  5.41 us
    all_to_all x1, waiting for transfers between devices, per_device(): latents = lax.all_to_all(copies, 'tm', 0, 0, tiled=True)  3.68 us
    pallas_call x1, Pallas kernels, per_device(): call(fold_kernel, [struct((inputs, 2 * width), BF16), struct((2 * width,...  3.68 us
    ppermute x1, starting transfers between devices, per_device(): lax.ppermute(own_pair, 'ctx', [(i, i ^ 1) for i in range(count)])  2.1 us
  transfers between devices with their start and end apart: 3, of which 2 were waited for; matrix products, arithmetic and copies ran while one was open for 0% of the time, Pallas kernels for 24%

profile of v5, /device:TPU:1, one launch (start us, length us, event | category | flops | bytes accessed | tf_op | source)
XLA Modules:
  0.0 60.2 jit_solution(13475346082197298568)
XLA Ops:
  0.0 0.0 copy-start.2
  0.0 0.0 copy-start.3
  0.0 0.8 %copy-done.3 = f32[1,96,64]{1,2,0:T(8,128)S(1)} copy-done((f32[1,96,64]{1,2,0:T(8,128)S(1)}, f32[1,96,64]{1,2,0:T(8,128)}, u32[]{:S(2)}) %copy-start.3) | copy-done | bytes 24600
  0.8 0.8 %shard_map.118 = bf16[16,48,128]{2,1,0:T(8,128)(2,1)} custom-call(f32[64,96]{1,0:T(8,128)S(1)} %bitcast.16), custom_call_target="tpu_custom_call" | custom-call | tf_op jit(solution)/shard_map/pallas_call | solution.py:246
  1.7 0.0 copy-start.6
  1.7 0.0 copy-start.5
  1.7 9.1 %all-to-all-start = ((bf16[16,48,128]{2,1,0:T(8,128)(2,1)}), bf16[16,48,128]{2,1,0:T(8,128)(2,1)S(1)}, u32[]{:S(2)}, u32[]{:S(2)}) async-start(bf16[16,48,128]{2,1,0:T(8,128)(2,1)} %shard_map.118), calls=%async_computation | async-start | bytes 393216 | tf_op jit(solution)/shard_map/all_to_all | solution.py:247
  10.8 0.0 copy-start.4
  10.8 0.0 copy-done.6
  10.9 0.1 fusion
  11.0 0.1 pad_maximum_fusion.feature_ref
  11.1 0.0 copy-start.7
  11.1 0.0 copy-start.8
  11.1 0.0 copy-done.2
  11.1 0.0 copy-done.5
  11.1 0.5 copy-done.4
  11.6 0.1 copy-done.7
  11.7 0.0 copy-done.8
  11.7 0.0 copy-start
  11.7 0.0 copy-start.9
  11.7 0.0 copy-start.10
  11.8 3.7 %shard_map.119 = (bf16[256,256]{1,0:T(8,128)(2,1)S(1)}, bf16[256,128]{1,0:T(8,128)(2,1)S(1)}, f32[48,128]{1,0:T(8,128)S(1)}, f32[2,128]{1,0:T(2,128)S(1)}, f32[16,128]{1,0:T(8,128)S(1)}) custom-call(s32[17]{0:T(128)S(1)} %copy-done.6, bf16[16,128]{1,0:T(8,128)(2,1)S(1)} %pad_maximum_fusion.feature_ref, f32[64,96]{1,0:T(8,128)S(1)} %bitcast.17, ...), custom_call_target="tpu_custom_call" | custom-call | flops 1048576 | bytes 1024 | tf_op jit(solution)/shard_map/pallas_call | solution.py:251
  15.4 3.7 %all-to-all-done.latent_ref = bf16[16,48,128]{2,1,0:T(8,128)(2,1)S(1)} async-done(((bf16[16,48,128]{2,1,0:T(8,128)(2,1)}), bf16[16,48,128]{2,1,0:T(8,128)(2,1)S(1)}, u32[]{:S(2)}, u32[]{:S(2)}) %all-to-all-start) | async-done | bytes 196640 | tf_op jit(solution)/shard_map/all_to_all | solution.py:247
  19.1 11.0 %collective-permute-start.1 = (bf16[16,48,128]{2,1,0:T(8,128)(2,1)S(1)}, bf16[16,48,128]{2,1,0:T(8,128)(2,1)S(1)}, u32[]{:S(2)}, u32[]{:S(2)}) collective-permute-start(bf16[16,48,128]{2,1,0:T(8,128)(2,1)S(1)} %all-to-all-done.latent_ref), channel_id=1, source_target_pairs={{1,2},{2,1},{3,4},{4,3},{5,6},{6,5},{7,8},{8,7},{9,10},{10,9},{11,... | collective-permute-start | bytes 589832 | tf_op jit(solution)/shard_map/ppermute | solution.py:249
  30.1 0.0 copy-done
  30.1 0.0 copy-done.9
  30.1 0.0 copy-done.10
  30.1 0.0 copy-start.1
  30.1 5.5 %shard_map.120 = (bf16[1536,128]{1,0:T(8,128)(2,1)S(1)}, bf16[1536,256]{1,0:T(8,128)(2,1)S(1)}) custom-call(bf16[16,48,128]{2,1,0:T(8,128)(2,1)S(1)} %all-to-all-done.latent_ref, bf16[16,128]{1,0:T(8,128)(2,1)S(1)} %pad_maximum_fusion.feature_ref, bf16[128,3072]{1,0:T(8,128)(2,1)S(1)} %copy-done, bf16[64,3072]{1,0:T(8,128)(2,1)S(1)} %copy-done.2, ...), custom_call_target="tpu_custom_call" | custom-call | flops 48318382080 | bytes 4194304 | tf_op jit(solution)/shard_map/pallas_call | solution.py:284
  35.6 2.1 %collective-permute-start = (bf16[1536,256]{1,0:T(8,128)(2,1)S(1)}, bf16[1536,256]{1,0:T(8,128)(2,1)S(1)}, u32[]{:S(2)}, u32[]{:S(2)}) collective-permute-start(bf16[1536,256]{1,0:T(8,128)(2,1)S(1)} %get-tuple-element.15.own_ref), channel_id=1, source_target_pairs={{0,1},{1,0},{2,3},{3,2},{4,5},{5,4},{6,7},{7,6},{8,9},{9,8},{10,11... | collective-permute-start | bytes 2359304 | tf_op jit(solution)/shard_map/ppermute | solution.py:291
  37.7 1.7 %collective-permute-done.1.latent_ref = bf16[16,48,128]{2,1,0:T(8,128)(2,1)S(1)} collective-permute-done((bf16[16,48,128]{2,1,0:T(8,128)(2,1)S(1)}, bf16[16,48,128]{2,1,0:T(8,128)(2,1)S(1)}, u32[]{:S(2)}, u32[]{:S(2)}) %collective-permute-start.1) | collective-permute-done | bytes 196640 | tf_op jit(solution)/shard_map/ppermute | solution.py:249
  39.5 0.0 copy-done.1
  39.5 5.4 %shard_map.121.outer_ref = bf16[1536,256]{1,0:T(8,128)(2,1)S(1)} custom-call(bf16[16,48,128]{2,1,0:T(8,128)(2,1)S(1)} %collective-permute-done.1.latent_ref, bf16[16,128]{1,0:T(8,128)(2,1)S(1)} %pad_maximum_fusion.feature_ref, bf16[128,3072]{1,0:T(8,128)(2,1)S(1)} %copy-done, bf16[64,3072]{1,0:T(8,128)(2,1)S(1)} %copy-done.2, ...), custom_call_target="tpu_custom_call" | custom-call | flops 48318382080 | bytes 4194304 | tf_op jit(solution)/shard_map/pallas_call | solution.py:292
  44.9 0.0 collective-permute-done.inner_ref
  44.9 1.8 %shard_map.122 = bf16[16,48,128]{2,1,0:T(8,128)(2,1)S(1)} custom-call(bf16[1536,128]{1,0:T(8,128)(2,1)S(1)} %get-tuple-element.14.query_ref, bf16[1536,256]{1,0:T(8,128)(2,1)S(1)} %get-tuple-element.15.own_ref, bf16[1536,256]{1,0:T(8,128)(2,1)S(1)} %collective-permute-done.inner_ref, bf16[1536,256]{1,0:T(8,128)(2,1)S(1)} %shard_map.121.outer_ref, ...), custom_call_target="tpu_custom_call" | custom-call | flops 6039797760 | bytes 4194304 | tf_op jit(solution)/shard_map/pallas_call | solution.py:299
  46.7 12.7 %all_to_all.10.taken_ref = bf16[16,48,128]{2,1,0:T(8,128)(2,1)S(1)} all-to-all(bf16[16,48,128]{2,1,0:T(8,128)(2,1)S(1)} %shard_map.122), channel_id=1, replica_groups=mesh['tm'=16,'ctx'=32] {'tm'}, dimensions={0} | all-to-all | bytes 393216 | tf_op jit(solution)/shard_map/all_to_all | solution.py:307
  59.5 0.8 %shard_map.123 = f32[64,96]{1,0:T(8,128)} custom-call(bf16[16,48,128]{2,1,0:T(8,128)(2,1)S(1)} %all_to_all.10.taken_ref, bf16[16,48,128]{2,1,0:T(8,128)(2,1)S(1)} %all-to-all-done.latent_ref), custom_call_target="tpu_custom_call" | custom-call | tf_op jit(solution)/shard_map/pallas_call | solution.py:308
  (2 shorter events, 0.0 us)
Async XLA Ops:
  0.0 11.1 %copy-start.2 = (bf16[64,3072]{1,0:T(8,128)(2,1)S(1)}, bf16[64,3072]{1,0:T(8,128)(2,1)}, u32[]{:S(2)}) copy-start(bf16[64,3072]{1,0:T(8,128)(2,1)} %embed_ref.3) | copy-start | bytes 1179652
  0.0 0.8 %copy-start.3 = (f32[1,96,64]{1,2,0:T(8,128)S(1)}, f32[1,96,64]{1,2,0:T(8,128)}, u32[]{:S(2)}) copy-start(f32[1,96,64]{1,2,0:T(8,128)} %param.12) | copy-start | bytes 73732
  1.7 9.2 %copy-start.6 = (s32[17]{0:T(128)S(1)}, s32[17]{0:T(128)}, u32[]{:S(2)}) copy-start(s32[17]{0:T(128)} %plan_ref.1) | copy-start | bytes 208
  1.7 9.4 %copy-start.5 = (f32[1,96,64]{1,2,0:T(8,128)S(1)}, f32[1,96,64]{1,2,0:T(8,128)}, u32[]{:S(2)}) copy-start(f32[1,96,64]{1,2,0:T(8,128)} %param.13) | copy-start | bytes 73732
  1.7 17.5 %all-to-all-start = ((bf16[16,48,128]{2,1,0:T(8,128)(2,1)}), bf16[16,48,128]{2,1,0:T(8,128)(2,1)S(1)}, u32[]{:S(2)}, u32[]{:S(2)}) async-start(bf16[16,48,128]{2,1,0:T(8,128)(2,1)} %shard_map.118), calls=%async_computation | async-start | bytes 393216 | tf_op jit(solution)/shard_map/all_to_all | solution.py:247
  10.8 0.8 %copy-start.4 = (f32[1,96,64]{1,2,0:T(8,128)S(1)}, f32[1,96,64]{1,2,0:T(8,128)}, u32[]{:S(2)}) copy-start(f32[1,96,64]{1,2,0:T(8,128)} %param.12) | copy-start | bytes 73732
  11.1 0.7 %copy-start.7 = (f32[1,128]{1,0:T(1,128)S(1)}, f32[1,128]{1,0:T(1,128)}, u32[]{:S(2)}) copy-start(f32[1,128]{1,0:T(1,128)} %gain_query_hbm.1) | copy-start | bytes 1540
  11.1 0.7 %copy-start.8 = (f32[1,128]{1,0:T(1,128)S(1)}, f32[1,128]{1,0:T(1,128)}, u32[]{:S(2)}) copy-start(f32[1,128]{1,0:T(1,128)} %gain_key_hbm.1) | copy-start | bytes 1540
  11.7 18.4 %copy-start = (bf16[128,3072]{1,0:T(8,128)(2,1)S(1)}, bf16[128,3072]{1,0:T(8,128)(2,1)}, u32[]{:S(2)}) copy-start(bf16[128,3072]{1,0:T(8,128)(2,1)} %time_ref.3) | copy-start | bytes 2359300
  11.7 18.4 %copy-start.9 = (bf16[1,3072,128]{2,1,0:T(8,128)(2,1)S(1)}, bf16[1,3072,128]{2,1,0:T(8,128)(2,1)}, u32[]{:S(2)}) copy-start(bf16[1,3072,128]{2,1,0:T(8,128)(2,1)} %param.17) | copy-start | bytes 2359300
  11.7 18.4 %copy-start.10 = (bf16[1,3072,128]{2,1,0:T(8,128)(2,1)S(1)}, bf16[1,3072,128]{2,1,0:T(8,128)(2,1)}, u32[]{:S(2)}) copy-start(bf16[1,3072,128]{2,1,0:T(8,128)(2,1)} %param.18) | copy-start | bytes 2359300
  19.1 20.4 %collective-permute-start.1 = (bf16[16,48,128]{2,1,0:T(8,128)(2,1)S(1)}, bf16[16,48,128]{2,1,0:T(8,128)(2,1)S(1)}, u32[]{:S(2)}, u32[]{:S(2)}) collective-permute-start(bf16[16,48,128]{2,1,0:T(8,128)(2,1)S(1)} %all-to-all-done.latent_ref), channel_id=1, source_target_pairs={{1,2},{2,1},{3,4},{4,3},{5,6},{6,5},{7,8},{8,7},{9,10},{10,9},{11,... | collective-permute-start | bytes 589832 | tf_op jit(solution)/shard_map/ppermute | solution.py:249
  30.1 9.4 %copy-start.1 = (bf16[1,3072,128]{2,1,0:T(8,128)(2,1)S(1)}, bf16[1,3072,128]{2,1,0:T(8,128)(2,1)}, u32[]{:S(2)}) copy-start(bf16[1,3072,128]{2,1,0:T(8,128)(2,1)} %param.19) | copy-start | bytes 2359300
  35.6 9.3 %collective-permute-start = (bf16[1536,256]{1,0:T(8,128)(2,1)S(1)}, bf16[1536,256]{1,0:T(8,128)(2,1)S(1)}, u32[]{:S(2)}, u32[]{:S(2)}) collective-permute-start(bf16[1536,256]{1,0:T(8,128)(2,1)S(1)} %get-tuple-element.15.own_ref), channel_id=1, source_target_pairs={{0,1},{1,0},{2,3},{3,2},{4,5},{5,4},{6,7},{7,6},{8,9},{9,8},{10,11... | collective-permute-start | bytes 2359304 | tf_op jit(solution)/shard_map/ppermute | solution.py:291
